TPU v7x, 32 devices: a whole 2x2x4 slice. The times are simulated.
32 devices in a mesh: dp: 8 (over z, x), mp: 4 (over y, core).
Axes of the slice: x: 2, y: 2, z: 4, core: 2. Of those that a mesh axis runs over, the one named last changes fastest.
Arguments:
- tokens: bfloat16 [16384, 1024], P(('dp', 'mp')), may hold values from -6 to 6
- condition: bfloat16 [64, 768], P(('dp', 'mp')), may hold values from -6 to 6
- buckets: int32 [64], P(('dp', 'mp')), may hold values from 0 to 15
- heads_weight: bfloat16 [1024, 3, 1024], P(None, None, 'mp'), may hold values from -0.1875 to 0.1875
- merge_weight: bfloat16 [1024, 1024], P('mp'), may hold values from -1.5 to 1.5
- expand_weight: bfloat16 [1024, 2, 3072], P(None, None, 'mp'), may hold values from -0.1875 to 0.1875
- reduce_weight: bfloat16 [3072, 1024], P('mp'), may hold values from -0.109375 to 0.109375
- adapt_first: bfloat16 [768, 1024], replicated, may hold values from -0.109375 to 0.109375
- adapt_second: bfloat16 [768, 1024], replicated, may hold values from -0.109375 to 0.109375
- cosine_scale: float32 [16], P('mp'), may hold values from 8 to 24
- cotangent: bfloat16 [16384, 1024], P(('dp', 'mp')), may hold values from -6 to 6
Outputs:
- layer_out: float32 [16384, 1024], P(('dp', 'mp'))
- tokens_grad: float32 [16384, 1024], P(('dp', 'mp'))
- condition_grad: float32 [64, 768], P(('dp', 'mp'))
- heads_grad: float32 [1024, 3, 1024], P(None, None, 'mp')
- merge_grad: float32 [1024, 1024], P('mp')
- expand_grad: float32 [1024, 2, 3072], P(None, None, 'mp')
- reduce_grad: float32 [3072, 1024], P('mp')
- first_grad: float32 [768, 1024], replicated
- second_grad: float32 [768, 1024], replicated
- cosine_grad: float32 [16], P('mp')
All inputs are finite; a program needn't handle non-finite values.
Results may differ from a plain program's by a relative error of at most 0.025.
Values may be sent and summed in bfloat16 or wider, within the bound.
No kernel may reach another device: no remote copies, remote signals or barrier semaphores. Data moves between devices by JAX's collectives and lax.ppermute only.
A program may use at most 192 MiB of HBM per device.

v0:
```python
import jax
import jax.numpy as jnp
import numpy as np
from jax import lax
from jax.sharding import PartitionSpec as P

HEAD_DIM = 64
BUCKET = 256


epsilon = 1e-06
GRID_ROWS = np.array([16, 12, 21, 14, 18, 12, 16, 10, 20, 8, 24, 11, 22, 8, 32, 13], np.int32)
GRID_COLS = np.array([16, 21, 12, 18, 14, 16, 12, 20, 10, 24, 8, 22, 11, 32, 8, 13], np.int32)
contract_rows = (((0,), (0,)), ((), ()))
contract_last = (((1,), (1,)), ((), ()))


def grid_lookup(bucket_ids):
    choose = (bucket_ids[:, None] == jnp.arange(16, dtype=jnp.int32)[None, :]).astype(jnp.int32)
    heights = jnp.sum(choose * jnp.asarray(GRID_ROWS)[None, :], axis=1)
    widths = jnp.sum(choose * jnp.asarray(GRID_COLS)[None, :], axis=1)
    places = jnp.arange(BUCKET, dtype=jnp.int32)[None, :]
    row_pos = places // widths[:, None]
    col_pos = places % widths[:, None]
    valid = places < (heights * widths)[:, None]
    quarter = HEAD_DIM // 8
    freqs = 10000.0 ** (-jnp.arange(quarter, dtype=jnp.float32) / quarter)
    angles = jnp.concatenate(
        [
            row_pos.astype(jnp.float32)[..., None] * freqs,
            col_pos.astype(jnp.float32)[..., None] * freqs,
        ],
        -1,
    )
    return (jnp.cos(angles), jnp.sin(angles), valid)


def rotate(values, cosines, sines):
    half = HEAD_DIM // 4
    first = values[..., :half]
    second = values[..., half : 2 * half]
    return jnp.concatenate(
        [
            first * cosines - second * sines,
            first * sines + second * cosines,
            values[..., 2 * half :],
        ],
        -1,
    )


def shape_heads(raw, scale, cosines, sines):
    normed = (
        raw * lax.rsqrt(jnp.sum(raw * raw, -1, keepdims=True) + epsilon) * jnp.sqrt(scale)[:, None]
    )
    return rotate(normed, cosines, sines)


def rms_adapt(values, product):
    return (
        values
        * lax.rsqrt(jnp.mean(values * values, -1, keepdims=True) + epsilon)
        * (1.0 + product[:, None, :])
    )


def geglu(gate_up):
    half = gate_up.shape[-1] // 2
    return jax.nn.gelu(gate_up[:, :half], approximate=True) * gate_up[:, half:]


def per_device(
    tokens,
    condition,
    buckets,
    heads_weight,
    merge_weight,
    expand_weight,
    reduce_weight,
    adapt_first,
    adapt_second,
    cosine_scale,
    cotangent,
):
    width = tokens.shape[1]
    local_images = buckets.shape[0]
    own_rows = tokens.shape[0]
    local_heads = cosine_scale.shape[0]
    heads_flat = heads_weight.reshape(width, -1)
    expand_flat = expand_weight.reshape(width, -1)
    image_shape = (local_images, BUCKET, width)
    tokens_full = tokens.astype(jnp.float32).reshape(image_shape)
    first_prod = jnp.dot(condition, adapt_first, preferred_element_type=jnp.float32)
    second_prod = jnp.dot(condition, adapt_second, preferred_element_type=jnp.float32)
    first_normed, first_back = jax.vjp(rms_adapt, tokens_full, first_prod)
    first_low = first_normed.reshape(own_rows, width).astype(jnp.bfloat16)
    gathered, group_ids = (
        lax.all_gather(first_low, "mp", axis=0, tiled=True),
        lax.all_gather(buckets, "mp", axis=0, tiled=True),
    )
    group_rows = gathered.shape[0]
    group_images = group_ids.shape[0]
    cosines, sines, valid = grid_lookup(group_ids)
    cosines = cosines.reshape(group_rows, 1, -1)
    sines = sines.reshape(group_rows, 1, -1)
    triple = jnp.dot(gathered, heads_flat, preferred_element_type=jnp.float32)
    triple = triple.reshape(group_rows, 3, local_heads, HEAD_DIM)

    def shape_pair(raw_query, raw_key, scale):
        return (
            shape_heads(raw_query, scale, cosines, sines),
            shape_heads(raw_key, scale, cosines, sines),
        )

    (query_full, key_full), shape_back = jax.vjp(
        shape_pair, triple[:, 0], triple[:, 1], cosine_scale
    )
    head_shape = (group_images, BUCKET, local_heads, HEAD_DIM)
    queries = query_full.astype(jnp.bfloat16).reshape(head_shape)
    key_rows = key_full.astype(jnp.bfloat16).reshape(head_shape)
    value_rows = triple[:, 2].astype(jnp.bfloat16).reshape(head_shape)
    scores = jnp.einsum("ithd,ishd->ihts", queries, key_rows, preferred_element_type=jnp.float32)
    scores = jnp.where(valid[:, None, None, :], scores, -1e30)
    probs = jax.nn.softmax(scores, axis=-1)
    probs_low = probs.astype(jnp.bfloat16)
    mixed = jnp.einsum("ihts,ishd->ithd", probs_low, value_rows, preferred_element_type=jnp.float32)
    mixed_low = mixed.astype(jnp.bfloat16).reshape(group_rows, local_heads * HEAD_DIM)
    attend_sum = lax.psum_scatter(
        jnp.dot(mixed_low, merge_weight, preferred_element_type=jnp.float32),
        "mp",
        scatter_dimension=0,
        tiled=True,
    )
    middle = tokens_full + attend_sum.reshape(image_shape)
    second_normed, second_back = jax.vjp(rms_adapt, middle, second_prod)
    second_low = second_normed.reshape(own_rows, width).astype(jnp.bfloat16)
    gate_up = jnp.dot(
        lax.all_gather(second_low, "mp", axis=0, tiled=True),
        expand_flat,
        preferred_element_type=jnp.float32,
    )
    hidden_full, geglu_back = jax.vjp(geglu, gate_up)
    hidden_low = hidden_full.astype(jnp.bfloat16)
    mixer_sum = lax.psum_scatter(
        jnp.dot(hidden_low, reduce_weight, preferred_element_type=jnp.float32),
        "mp",
        scatter_dimension=0,
        tiled=True,
    )
    layer_out = (middle + mixer_sum.reshape(image_shape)).reshape(own_rows, width)
    out_group = lax.all_gather(cotangent, "mp", axis=0, tiled=True)
    reduce_local = lax.dot_general(
        hidden_low, out_group, contract_rows, preferred_element_type=jnp.float32
    )
    hidden_grad = lax.dot_general(
        out_group, reduce_weight, contract_last, preferred_element_type=jnp.float32
    )
    (gate_up_grad,) = geglu_back(hidden_grad)
    gate_up_low = gate_up_grad.astype(jnp.bfloat16)
    partner = gate_up_low
    expand_local = lax.dot_general(
        lax.all_gather(second_low, "mp", axis=0, tiled=True),
        partner,
        contract_rows,
        preferred_element_type=jnp.float32,
    )
    second_grad_in = lax.psum_scatter(
        lax.dot_general(
            gate_up_low, expand_flat, contract_last, preferred_element_type=jnp.float32
        ),
        "mp",
        scatter_dimension=0,
        tiled=True,
    )
    middle_part, second_prod_grad = second_back(second_grad_in.reshape(image_shape))
    middle_grad = cotangent.astype(jnp.float32).reshape(image_shape) + middle_part
    attend_low = middle_grad.reshape(own_rows, width).astype(jnp.bfloat16)
    attend_group = lax.all_gather(attend_low, "mp", axis=0, tiled=True)
    merge_local = lax.dot_general(
        mixed_low, attend_group, contract_rows, preferred_element_type=jnp.float32
    )
    mixed_grad = lax.dot_general(
        attend_group, merge_weight, contract_last, preferred_element_type=jnp.float32
    )
    mixed_grad_low = mixed_grad.astype(jnp.bfloat16).reshape(head_shape)
    probs_grad = jnp.einsum(
        "ithd,ishd->ihts", mixed_grad_low, value_rows, preferred_element_type=jnp.float32
    )
    value_grad = jnp.einsum(
        "ihts,ithd->ishd", probs_low, mixed_grad_low, preferred_element_type=jnp.float32
    )
    scores_grad = probs * (probs_grad - jnp.sum(probs_grad * probs, -1, keepdims=True))
    scores_low = scores_grad.astype(jnp.bfloat16)
    query_grad = jnp.einsum(
        "ihts,ishd->ithd", scores_low, key_rows, preferred_element_type=jnp.float32
    )
    key_grad = jnp.einsum(
        "ihts,ithd->ishd", scores_low, queries, preferred_element_type=jnp.float32
    )
    flat_heads = (group_rows, local_heads, HEAD_DIM)
    raw_query_grad, raw_key_grad, scale_local = shape_back(
        (query_grad.reshape(flat_heads), key_grad.reshape(flat_heads))
    )
    triple_grad = jnp.stack([raw_query_grad, raw_key_grad, value_grad.reshape(flat_heads)], axis=1)
    triple_low = triple_grad.reshape(group_rows, -1).astype(jnp.bfloat16)
    partner = triple_low
    heads_local = lax.dot_general(
        lax.all_gather(first_low, "mp", axis=0, tiled=True),
        partner,
        contract_rows,
        preferred_element_type=jnp.float32,
    )
    first_grad_in = lax.psum_scatter(
        lax.dot_general(triple_low, heads_flat, contract_last, preferred_element_type=jnp.float32),
        "mp",
        scatter_dimension=0,
        tiled=True,
    )
    tokens_part, first_prod_grad = first_back(first_grad_in.reshape(image_shape))
    tokens_grad = (middle_grad + tokens_part).reshape(own_rows, width)
    first_prod_low = first_prod_grad.astype(jnp.bfloat16)
    second_prod_low = second_prod_grad.astype(jnp.bfloat16)
    condition_grad = lax.dot_general(
        first_prod_low, adapt_first, contract_last, preferred_element_type=jnp.float32
    ) + lax.dot_general(
        second_prod_low, adapt_second, contract_last, preferred_element_type=jnp.float32
    )
    first_local = lax.dot_general(
        condition, first_prod_low, contract_rows, preferred_element_type=jnp.float32
    )
    second_local = lax.dot_general(
        condition, second_prod_low, contract_rows, preferred_element_type=jnp.float32
    )
    first_total, second_total = lax.psum((first_local, second_local), ("dp", "mp"))
    heads_total, merge_total, expand_total, reduce_total, scale_total = lax.psum(
        (heads_local, merge_local, expand_local, reduce_local, scale_local), "dp"
    )
    return (
        layer_out,
        tokens_grad,
        condition_grad,
        heads_total.reshape(width, 3, local_heads * HEAD_DIM),
        merge_total,
        expand_total.reshape(width, 2, -1),
        reduce_total,
        first_total,
        second_total,
        scale_total,
    )


def solution(mesh):
    return jax.shard_map(
        per_device,
        mesh=mesh,
        in_specs=(
            P(("dp", "mp"), None),
            P(("dp", "mp"), None),
            P(("dp", "mp")),
            P(None, None, "mp"),
            P("mp", None),
            P(None, None, "mp"),
            P("mp", None),
            P(),
            P(),
            P("mp"),
            P(("dp", "mp"), None),
        ),
        out_specs=(
            P(("dp", "mp"), None),
            P(("dp", "mp"), None),
            P(("dp", "mp"), None),
            P(None, None, "mp"),
            P("mp", None),
            P(None, None, "mp"),
            P("mp", None),
            P(),
            P(),
            P("mp"),
        ),
        check_vma=False,
    )
```

profile of v0, /device:TPU:0, one launch (start us, length us, event | category | flops | bytes accessed | tf_op | source)
XLA Modules:
  0.0 1184.7 jit_solution(11298829435202715124)
XLA Ops:
  7.2 1.7 fusion.15
  9.5 1.8 convolution_add_fusion.1
  11.9 1.3 fusion.21
  14.8 6.4 all-reduce.8
  21.8 2.7 copy.66
  25.2 25.3 %all-gather.5.cloned.1.call-done = bf16[2048,1024]{1,0:T(8,128)(2,1)} async-done(((bf16[512,1024]{1,0:T(8,128)(2,1)}), bf16[2048,1024]{1,0:T(8,128)(2,1)}) %all-gather.5.cloned.1.call-update) | async-done | bytes 4194320 | tf_op jit(solution)/shard_map/all_gather | solution.py:98
  50.5 5.7 fusion.10
  57.0 1.8 copy.104
  63.9 7.5 fusion.61
  72.0 4.6 fusion.33
  78.5 4.6 fusion.62
  83.7 1.7 convolution_add_fusion
  85.5 69.5 %reduce-scatter.5.cloned.1.call-done = f32[512,1024]{1,0:T(8,128)} async-done(((f32[2048,1024]{1,0:T(8,128)}), f32[512,1024]{1,0:T(8,128)}) %reduce-scatter.5.cloned.1.call-update) | async-done | bytes 2097168 | tf_op jit(solution)/shard_map/reduce_scatter | solution.py:128
  155.0 2.1 multiply_reduce_fusion.8
  157.6 1.3 fusion.22
  160.0 4.1 copy.109
  164.1 29.5 %all-gather.7.cloned.1.call-done = bf16[2048,1024]{1,0:T(8,128)(2,1)} async-done(((bf16[512,1024]{1,0:T(8,128)(2,1)}), bf16[2048,1024]{1,0:T(8,128)(2,1)}) %all-gather.7.cloned.1.call-update) | async-done | bytes 4194320 | tf_op jit(solution)/shard_map/all_gather | solution.py:138
  193.6 12.3 %fusion.63 = f32[2048,1536]{1,0:T(8,128)} fusion(bf16[2048,1024]{1,0:T(8,128)(2,1)} %all-gather.7.cloned.1.call-done, bf16[1024,1536]{1,0:T(8,128)(2,1)} %bitcast.189), kind=kOutput, calls=%fused_computation.146 | convolution fusion | flops 6442450944 | bytes 19922944 | tf_op jit(solution)/shard_map/dot_general | solution.py:137
  206.0 23.7 %all-gather.9.cloned.1.call-done = bf16[2048,1024]{1,0:T(8,128)(2,1)} async-done(((bf16[512,1024]{1,0:T(8,128)(2,1)}), bf16[2048,1024]{1,0:T(8,128)(2,1)}) %all-gather.9.cloned.1.call-update) | async-done | bytes 4194320 | tf_op jit(solution)/shard_map/all_gather | solution.py:151
  229.7 15.6 %fusion.14 = (f32[2048,768]{1,0:T(8,128)S(1)}, f32[2048,768]{1,0:T(8,128)}, bf16[2048,768]{1,0:T(8,128)(2,1)}) fusion(f32[2048,1536]{1,0:T(8,128)} %fusion.63, bf16[2048,1024]{1,0:T(8,128)(2,1)} %all-gather.9.cloned.1.call-done, bf16[768,1024]{1,0:T(8,128)(2,1)S(1)} %copy-done), kind=kOutput, calls=%fused_computation.37 | convolution fusion | flops 3258974208 | bytes 34078720 | tf_op jit(solution)/shard_map/dot_general | solution.py:155
  245.2 2.7 copy-done.48
  247.9 10.8 fusion.40
  258.8 71.8 %reduce-scatter.9.cloned.1.call-done = f32[512,1024]{1,0:T(8,128)} async-done(((f32[2048,1024]{1,0:T(8,128)}), f32[512,1024]{1,0:T(8,128)}) %reduce-scatter.9.cloned.1.call-update) | async-done | bytes 2097168 | tf_op jit(solution)/shard_map/reduce_scatter | solution.py:167
  330.7 2.8 multiply_reduce_fusion.7
  334.8 1.7 fusion.59
  336.7 34.4 %all-gather.11.cloned.1.call-done = bf16[2048,1024]{1,0:T(8,128)(2,1)} async-done(((bf16[512,1024]{1,0:T(8,128)(2,1)}), bf16[2048,1024]{1,0:T(8,128)(2,1)}) %all-gather.11.cloned.1.call-update) | async-done | bytes 4194320 | tf_op jit(solution)/shard_map/all_gather | solution.py:178
  371.1 4.5 convolution_convert_fusion
  375.5 4.4 reshape.447
  379.9 4.0 copy.77
  383.9 5.2 fusion.27
  389.2 4.5 multiply_reduce_fusion
  393.9 1.8 multiply_convert_fusion
  395.7 1.4 convolution_bitcast_fusion.2
  397.1 2.1 convolution_bitcast_fusion.3
  399.7 1.0 split.27
  400.7 1.3 multiply_add_fusion.3
  403.0 1.6 copy.85
  404.6 2.3 stack_reshape.3
  407.0 4.1 multiply_reduce_fusion.2
  411.2 2.8 fusion.18
  414.4 1.7 copy-done.17
  416.1 5.7 fusion.65
  422.1 7.6 fusion.64
  430.3 63.3 %reduce-scatter.11.cloned.1.call-done = f32[512,1024]{1,0:T(8,128)} async-done(((f32[2048,1024]{1,0:T(8,128)}), f32[512,1024]{1,0:T(8,128)}) %reduce-scatter.11.cloned.1.call-update) | async-done | bytes 2097168 | tf_op jit(solution)/shard_map/reduce_scatter | solution.py:213
  493.7 3.5 multiply_reduce_fusion.3
  497.2 2.2 convolution_bitcast_fusion
  499.4 2.4 convolution_bitcast_fusion.1
  501.9 16.3 %fusion.39 = f32[1024,1536]{1,0:T(8,128)} fusion(bf16[2048,1024]{1,0:T(8,128)(2,1)} %all-gather.7.cloned.1.call-done, f32[2048,768]{1,0:T(8,128)} %get-tuple-element.59, f32[2048,768]{1,0:T(8,128)} %copy-done.48), kind=kOutput, calls=%fused_computation.82 | convolution fusion | flops 6448742400 | bytes 23068672 | tf_op jit(solution)/shard_map/dot_general | solution.py:161
  518.2 8.3 reshape.440
  526.4 8.6 fusion.67
  535.1 5.1 fusion.68
  540.2 3.6 copy.86
  543.8 4.8 fusion.66
  549.3 22.2 %psum.55 = f32[4]{0:T(128)} all-reduce(f32[4]{0:T(128)S(1)} %divide_multiply_fusion), channel_id=1, replica_groups=mesh['dp'=8,'mp'=4] {'dp'}, use_global_device_ids=true, to_apply=%region_27.28 | all-reduce | flops 4 | bytes 32 | tf_op jit(solution)/shard_map/psum | solution.py:235
  571.4 1.9 fusion.16
  573.4 5.9 fusion.20
  579.9 1.1 convolution_add_fusion.2
  581.0 149.1 %all-reduce.14.cloned.1.call-done = (f32[768,1024]{0,1:T(8,128)}, f32[768,1024]{0,1:T(8,128)}) async-done(((f32[768,1024]{0,1:T(8,128)}, f32[768,1024]{0,1:T(8,128)}), (f32[768,1024]{0,1:T(8,128)}, f32[768,1024]{0,1:T(8,128)})) %all-reduce.14.cloned.1.call-update) | async-done | bytes 6291472 | tf_op jit(solution)/shard_map/psum | solution.py:234
  730.1 3.5 copy.87
  733.6 3.5 copy.88
  737.2 425.9 %all-reduce.16.cloned.1.call-done = (f32[1024,3,256]{2,0,1:T(8,128)}, f32[256,1024]{1,0:T(8,128)}, f32[1024,2,768]{2,1,0:T(2,128)}, f32[768,1024]{1,0:T(8,128)}) async-done(((f32[1024,3,256]{2,0,1:T(8,128)}, f32[256,1024]{1,0:T(8,128)}, f32[1024,2,768]{2,1,0:T(2,128)}, f32[768,1024]{1,0:T(8,128)}), (f32[1024,3,256]{2,0,1:T(8,128)}, f32[256,1024]{1,0:T(8,128)}, f32[1024,2,768]{2,1,0:T(2,128)}, ...) | async-done | bytes 13631504 | tf_op jit(solution)/shard_map/psum | solution.py:235
  1163.1 3.8 copy.133
  1167.9 7.8 copy.135
  1175.7 1.7 copy.136
  (174 shorter events, 20.9 us)
Async XLA Ops:
  7.2 222.5 %copy-start = (bf16[768,1024]{1,0:T(8,128)(2,1)S(1)}, bf16[768,1024]{1,0:T(8,128)(2,1)}, u32[]{:S(2)}) copy-start(bf16[768,1024]{1,0:T(8,128)(2,1)} %param.19) | copy-start | bytes 4718596
  7.2 4.7 copy-start.1
  7.2 43.3 %all-gather.5.cloned.1.call-start = ((), (), s32[]{:S(2)}) async-start(), calls=%async_computation.4 | async-start | bytes 5242880 | tf_op jit(solution)/shard_map/all_gather | solution.py:98
  8.9 0.6 copy-start.34
  9.5 1.8 copy-start.32
  9.5 3.8 copy-start.47
  9.5 5.0 copy-start.46
  9.5 11.7 copy-start.43
  9.5 11.7 copy-start.41
  9.5 11.7 copy-start.42
  11.3 0.6 copy-start.27
  13.2 141.7 %reduce-scatter.5.cloned.1.call-start = ((), (), s32[]{:S(2)}) async-start(), calls=%async_computation.5 | async-start | bytes 10485760 | tf_op jit(solution)/shard_map/reduce_scatter | solution.py:128
  21.2 37.6 %copy-start.39 = (f32[4]{0:T(128)}, f32[4]{0:T(128)S(1)}, u32[]{:S(2)}) copy-start(f32[4]{0:T(128)S(1)} %sqrt.4) | copy-start | bytes 52
  56.3 2.9 copy-start.4
  62.9 1.0 copy-start.20
  71.4 0.6 copy-start.30
  76.6 1.9 copy-start.26
  77.5 1.0 copy-start.11
  83.0 0.7 copy-start.29
  83.1 110.6 %all-gather.7.cloned.1.call-start = ((), (), s32[]{:S(2)}) async-start(), calls=%async_computation.6 | async-start | bytes 5242880 | tf_op jit(solution)/shard_map/all_gather | solution.py:138
  155.0 2.7 copy-start.2
  157.0 0.6 copy-start.36
  159.0 70.7 %all-gather.9.cloned.1.call-start = ((), (), s32[]{:S(2)}) async-start(), calls=%async_computation.8 | async-start | bytes 5242880 | tf_op jit(solution)/shard_map/all_gather | solution.py:151
  159.6 171.1 %reduce-scatter.9.cloned.1.call-start = ((), (), s32[]{:S(2)}) async-start(), calls=%async_computation.9 | async-start | bytes 10485760 | tf_op jit(solution)/shard_map/reduce_scatter | solution.py:167
  229.7 18.3 %copy-start.19 = (bf16[128,8,2,768]{3,1,2,0:T(8,128)(2,1)S(1)}, bf16[128,8,2,768]{3,1,2,0:T(8,128)(2,1)}, u32[]{:S(2)}) copy-start(bf16[128,8,2,768]{3,1,2,0:T(8,128)(2,1)} %copy.109) | copy-start | bytes 9437188
  245.2 2.7 copy-start.48
  258.8 112.3 %all-gather.11.cloned.1.call-start = ((), (), s32[]{:S(2)}) async-start(), calls=%async_computation.10 | async-start | bytes 5242880 | tf_op jit(solution)/shard_map/all_gather | solution.py:178
  330.7 4.1 copy-start.3
  330.7 4.1 copy-start.5
  330.7 4.1 copy-start.8
  334.2 0.6 copy-start.37
  336.5 157.2 %reduce-scatter.11.cloned.1.call-start = ((), (), s32[]{:S(2)}) async-start(), calls=%async_computation.11 | async-start | bytes 10485760 | tf_op jit(solution)/shard_map/reduce_scatter | solution.py:213
  379.9 4.0 copy-start.31
  383.9 5.3 copy-start.23
  383.9 5.3 copy-start.24
  383.9 9.8 slice-start
  389.2 4.7 slice-start.1
  393.9 1.8 copy-start.21
  403.0 3.9 copy-start.40
  406.9 4.2 copy-start.6
  406.9 4.2 copy-start.7
  406.9 4.2 copy-start.12
  407.0 4.2 copy-start.13
  407.0 4.3 copy-start.14
  411.2 2.8 copy-start.15
  414.1 2.0 copy-start.22
  414.4 1.7 copy-start.17
  421.8 151.6 %reduce-scatter.7.cloned.1.call-start = ((), (), s32[]{:S(2)}) async-start(), calls=%async_computation.7 | async-start | bytes 10485760 | tf_op jit(solution)/shard_map/reduce_scatter | solution.py:144
  429.7 0.6 copy-start.33
  429.7 300.4 %all-reduce.14.cloned.1.call-start = ((), (), s32[]{:S(2)}) async-start(), calls=%async_computation.12 | async-start | bytes 12582912 | tf_op jit(solution)/shard_map/psum | solution.py:234
  501.8 661.3 %all-reduce.16.cloned.1.call-start = ((), (), s32[]{:S(2)}) async-start(), calls=%async_computation.13 | async-start | bytes 27262976 | tf_op jit(solution)/shard_map/psum | solution.py:235
  526.4 8.6 copy-start.18
  526.4 8.6 copy-start.45
  548.6 0.7 copy-start.44
  548.6 22.8 %copy-start.28 = (f32[2,1024]{1,0:T(2,128)S(1)}, f32[2,1024]{1,0:T(2,128)}, u32[]{:S(2)}) copy-start(f32[2,1024]{1,0:T(2,128)} %copy-done.27) | copy-start | bytes 24580
  548.6 24.7 %copy-start.35 = (f32[512]{0:T(512)S(1)}, f32[512]{0:T(512)}, u32[]{:S(2)}) copy-start(f32[512]{0:T(512)} %copy-done.34) | copy-start | bytes 6148
  548.6 24.8 %copy-start.38 = (f32[512]{0:T(512)S(1)}, f32[512]{0:T(512)}, u32[]{:S(2)}) copy-start(f32[512]{0:T(512)} %copy-done.37) | copy-start | bytes 6148
  573.4 5.9 copy-start.9
  573.4 6.4 copy-start.10
  1163.1 3.8 copy-start.25
  1167.9 7.8 copy-start.16
Sparse Core Ops, SparseCore 0:
  13.3 37.1 all-gather.4
  83.2 71.7 reduce-scatter.4
  159.1 34.4 all-gather.6
  195.1 34.4 all-gather.8
  258.9 71.7 reduce-scatter.8
  336.6 34.4 all-gather.10
  421.9 71.7 reduce-scatter.10
  496.4 71.6 reduce-scatter.6
  574.0 156.0 all-reduce.13
  736.2 426.8 all-reduce.15
where the time goes:
time: 1190 us; the launch traced here: 1180 us
  waiting for transfers between devices  893 us (75%)
  matrix products  137 us (12%)
  local copies, waits for them, and re-layouts  73 us (6%)
  other arithmetic  36.1 us (3%)
  blocking collectives  28.5 us (2%)
  between operations  15.9 us (1%)
    psum x1, waiting for transfers between devices, per_device(): lax.psum((heads_local, merge_local, expand_local, reduce_local, scale_loc...  426 us
    psum x1, waiting for transfers between devices, per_device(): lax.psum((first_local, second_local), ('dp', 'mp'))  149 us
    reduce_scatter x1, waiting for transfers between devices, per_device(): lax.psum_scatter(lax.dot_general(gate_up_low, expand_flat, contract_last,...  71.8 us
    reduce_scatter x1, waiting for transfers between devices, per_device(): lax.psum_scatter(jnp.dot(mixed_low, merge_weight, preferred_element_type=...  69.5 us
    reduce_scatter x1, waiting for transfers between devices, per_device(): lax.psum_scatter(lax.dot_general(triple_low, heads_flat, contract_last, p...  63.3 us
    unnamed x125, local copies, waits for them, and re-layouts  44.4 us
    all_gather x1, waiting for transfers between devices, per_device(): attend_group = lax.all_gather(attend_low, 'mp', axis=0, tiled=True)  34.4 us
    all_gather x1, waiting for transfers between devices, per_device(): lax.all_gather(second_low, 'mp', axis=0, tiled=True)  29.5 us
  transfers between devices with their start and end apart: 10, of which 9 were waited for; matrix products, arithmetic and copies ran while one was open for 9% of the time, Pallas kernels for 0%

commit v1 on v0

v1 whole, which is shorter than its diff:
```python
import functools

import jax
import jax.numpy as jnp
import numpy as np
from jax import lax
from jax.experimental import pallas as pl
from jax.experimental.pallas import tpu as pltpu
from jax.sharding import PartitionSpec as P

HEAD_DIM = 64
BUCKET = 256
EPS = 1e-06
NEG = -1e30
GRID_ROWS = np.array([16, 12, 21, 14, 18, 12, 16, 10, 20, 8, 24, 11, 22, 8, 32, 13], np.int32)
GRID_COLS = np.array([16, 21, 12, 18, 14, 16, 12, 20, 10, 24, 8, 22, 11, 32, 8, 13], np.int32)
F32 = jnp.float32
BF16 = jnp.bfloat16
VMEM_LIMIT = 56 * 1024 * 1024
GELU_A = float(np.sqrt(2.0 / np.pi))
GELU_B = 0.044715
CHUNK = 256


def nn(a, b):
    return lax.dot_general(a, b, (((1,), (0,)), ((), ())), preferred_element_type=F32)


def nt(a, b):
    return lax.dot_general(a, b, (((1,), (1,)), ((), ())), preferred_element_type=F32)


def tn(a, b):
    return lax.dot_general(a, b, (((0,), (0,)), ((), ())), preferred_element_type=F32)


def params():
    return pltpu.CompilerParams(vmem_limit_bytes=VMEM_LIMIT, dimension_semantics=("arbitrary",))


def cost(flops, nbytes, trans=0):
    return pl.CostEstimate(flops=int(flops), bytes_accessed=int(nbytes), transcendentals=int(trans))


def whole(shape):
    return pl.BlockSpec(shape, lambda i: (0,) * len(shape))


def rows(block, width):
    return pl.BlockSpec((block, width), lambda i: (i, 0))


def norm_first_kernel(x_ref, s_ref, out_ref):
    x = x_ref[...].astype(F32)
    r = lax.rsqrt(jnp.mean(x * x, -1, keepdims=True) + EPS)
    out_ref[...] = (x * r * s_ref[0]).astype(BF16)


def norm_first(tokens, scale):
    n, d = tokens.shape
    return pl.pallas_call(
        norm_first_kernel,
        grid=(n // BUCKET,),
        in_specs=[rows(BUCKET, d), pl.BlockSpec((1, 1, d), lambda i: (i, 0, 0))],
        out_specs=rows(BUCKET, d),
        out_shape=jax.ShapeDtypeStruct((n, d), BF16),
        compiler_params=params(),
        cost_estimate=cost(8 * n * d, 4 * n * d),
        name="norm_first",
    )(tokens, scale)


def norm_second_kernel(x_ref, part_ref, recv_ref, s_ref, mid_ref, out_ref):
    x = x_ref[...].astype(F32) + (part_ref[...] + recv_ref[...].astype(F32))
    mid_ref[...] = x
    r = lax.rsqrt(jnp.mean(x * x, -1, keepdims=True) + EPS)
    out_ref[...] = (x * r * s_ref[0]).astype(BF16)


def norm_second(tokens, part, recv, scale):
    n, d = tokens.shape
    return pl.pallas_call(
        norm_second_kernel,
        grid=(n // BUCKET,),
        in_specs=[rows(BUCKET, d)] * 3 + [pl.BlockSpec((1, 1, d), lambda i: (i, 0, 0))],
        out_specs=[rows(BUCKET, d)] * 2,
        out_shape=[jax.ShapeDtypeStruct((n, d), F32), jax.ShapeDtypeStruct((n, d), BF16)],
        compiler_params=params(),
        cost_estimate=cost(8 * n * d, 14 * n * d),
        name="norm_second",
    )(tokens, part, recv, scale)


def norm_back_kernel(extra, low, *refs):
    part_ref = refs[0]
    more = refs[1 : 1 + extra]
    x_ref, g_ref, s_ref = refs[1 + extra : 4 + extra]
    outs = refs[4 + extra :]
    grad = part_ref[...]
    for ref in more:
        grad = grad + ref[...].astype(F32)
    x = x_ref[...].astype(F32)
    r = lax.rsqrt(jnp.mean(x * x, -1, keepdims=True) + EPS)
    u = grad * s_ref[0]
    back = g_ref[...].astype(F32) + r * u - x * (r * r * r * jnp.mean(u * x, -1, keepdims=True))
    outs[0][...] = back
    outs[1][0] = jnp.sum(grad * x * r, 0, keepdims=True)
    if low:
        outs[2][...] = back.astype(BF16)


def norm_back(part, more, x, g, scale, low):
    n, d = x.shape
    per_image = pl.BlockSpec((1, 1, d), lambda i: (i, 0, 0))
    outs = [jax.ShapeDtypeStruct((n, d), F32), jax.ShapeDtypeStruct((n // BUCKET, 1, d), F32)]
    specs = [rows(BUCKET, d), per_image]
    if low:
        outs.append(jax.ShapeDtypeStruct((n, d), BF16))
        specs.append(rows(BUCKET, d))
    return pl.pallas_call(
        functools.partial(norm_back_kernel, len(more), low),
        grid=(n // BUCKET,),
        in_specs=[rows(BUCKET, d)] * (3 + len(more)) + [per_image],
        out_specs=specs,
        out_shape=outs,
        compiler_params=params(),
        cost_estimate=cost(16 * n * d, 18 * n * d),
        name="norm_back",
    )(part, *more, x, g, scale)


def head_sums(values, block_ones):
    high = values.astype(BF16)
    low = (values - high.astype(F32)).astype(BF16)
    return nn(high, block_ones) + nn(low, block_ones)


def partner(values):
    parts = []
    for start in range(0, values.shape[1], 128):
        part = values[:, start : start + 128]
        lane = lax.broadcasted_iota(jnp.int32, part.shape, 1) % HEAD_DIM
        parts.append(
            jnp.where(lane < HEAD_DIM // 4, pltpu.roll(part, 128 - 16, 1), pltpu.roll(part, 16, 1))
        )
    return jnp.concatenate(parts, 1)


def twice(table, width):
    return jnp.concatenate([table] * (width // table.shape[1]), 1)


def head_mask(shape, head):
    lane = lax.broadcasted_iota(jnp.int32, shape, 1)
    return (lane >= head * HEAD_DIM) & (lane < (head + 1) * HEAD_DIM)


def attend_forward_kernel(
    merge, heads, n_ref, w_ref, root_ref, ones_ref, cos_ref, sin_ref, bias_ref, *refs
):
    if merge:
        other_ref, m_own_ref, m_ref = refs[:3]
        refs = refs[3:]
    q_ref, k_ref, v_ref, cq_ref, ck_ref, mixed_ref = refs[:6]
    normed = n_ref[...]
    width = heads * HEAD_DIM
    cosines, sines = twice(cos_ref[...], width), twice(sin_ref[...], width)
    ones = ones_ref[...]
    root = root_ref[...]

    def shape_heads(which, c_ref):
        raw = nn(normed, w_ref[which])
        c = lax.rsqrt(head_sums(raw * raw, ones) + EPS) * root
        c_ref[...] = c
        n = raw * c
        return (n * cosines + partner(n) * sines).astype(BF16)

    q = shape_heads(0, cq_ref)
    k = shape_heads(1, ck_ref)
    v = nn(normed, w_ref[2]).astype(BF16)
    q_ref[...] = q
    k_ref[...] = k
    v_ref[...] = v
    bias = bias_ref[0]
    mixed = jnp.zeros((BUCKET, width), F32)
    for head in range(heads):
        mask = head_mask((BUCKET, width), head)
        zero = jnp.zeros_like(q)
        scores = nt(jnp.where(mask, q, zero), k) + bias
        e = jnp.exp(scores)
        probs = e * (1.0 / jnp.sum(e, -1, keepdims=True))
        mixed = mixed + nn(probs.astype(BF16), jnp.where(mask, v, zero))
    mixed = mixed.astype(BF16)
    mixed_ref[...] = mixed
    if merge:
        keep_ref, send_ref = refs[6:]
        part = nn(other_ref[...], m_own_ref[...]) + nn(mixed, m_ref[...])

        @pl.when(pl.program_id(0) < 2)
        def _():
            keep_ref[...] = part

        @pl.when(pl.program_id(0) >= 2)
        def _():
            send_ref[...] = part.astype(BF16)


def attend_forward(normed, weight, root, ones, cosines, sines, bias, merge=None):
    n, d = normed.shape
    width = weight.shape[2]
    images = n // BUCKET
    heads = width // HEAD_DIM
    half = images // 2
    block = rows(BUCKET, width)
    in_specs = [
        rows(BUCKET, d),
        whole(weight.shape),
        whole(root.shape),
        whole(ones.shape),
        rows(BUCKET, 128),
        rows(BUCKET, 128),
        pl.BlockSpec((1, 1, BUCKET), lambda i: (i, 0, 0)),
    ]
    operands = [normed, weight, root, ones, cosines, sines, bias]
    out_specs = [block] * 6
    outs = [jax.ShapeDtypeStruct((n, width), t) for t in (BF16, BF16, BF16, F32, F32, BF16)]
    flops = 2 * n * d * 3 * width + 4 * n * BUCKET * width * heads
    if merge is not None:
        other, own_weight, merge_weight = merge
        in_specs += [block, whole(own_weight.shape), whole(merge_weight.shape)]
        operands += [other, own_weight, merge_weight]
        out_specs += [
            pl.BlockSpec((BUCKET, d), lambda i: (jnp.minimum(i, half - 1), 0)),
            pl.BlockSpec((BUCKET, d), lambda i: (jnp.maximum(i - half, 0), 0)),
        ]
        outs += [
            jax.ShapeDtypeStruct((n // 2, d), F32),
            jax.ShapeDtypeStruct((n // 2, d), BF16),
        ]
        flops += 4 * n * width * d
    return pl.pallas_call(
        functools.partial(attend_forward_kernel, merge is not None, heads),
        grid=(images,),
        in_specs=in_specs,
        out_specs=out_specs,
        out_shape=outs,
        compiler_params=params(),
        cost_estimate=cost(flops * 2, 12 * 1024 * 1024, n * BUCKET * heads),
        name="attend_forward",
    )(*operands)


def attend_backward_kernel(
    second,
    heads,
    n_ref,
    w_ref,
    m_ref,
    inv_ref,
    ones_ref,
    cos_ref,
    sin_ref,
    valid_ref,
    b_ref,
    q_ref,
    k_ref,
    v_ref,
    cq_ref,
    ck_ref,
    mixed_ref,
    *refs,
):
    if second:
        prev_keep_ref, prev_send_ref = refs[:2]
        refs = refs[2:]
    hgrad_ref, mgrad_ref, scale_ref, keep_ref, send_ref, tg_ref, macc_ref = refs
    i = pl.program_id(0)
    width = heads * HEAD_DIM
    cosines, sines = twice(cos_ref[...], width), twice(sin_ref[...], width)
    ones = ones_ref[...]
    inv = inv_ref[...]
    branch = b_ref[...]
    q, k, v = q_ref[...], k_ref[...], v_ref[...]
    mixed = mixed_ref[...]
    dmix = nt(branch, m_ref[...]).astype(BF16)
    prod = (dmix.astype(F32) * mixed.astype(F32)).astype(BF16)
    bias = valid_ref[0]
    zero = jnp.zeros_like(q)
    dq = jnp.zeros((BUCKET, width), F32)
    dk = jnp.zeros((BUCKET, width), F32)
    dv = jnp.zeros((BUCKET, width), F32)
    for head in range(heads):
        mask = head_mask((BUCKET, width), head)
        qh = jnp.where(mask, q, zero)
        kh = jnp.where(mask, k, zero)
        dh = jnp.where(mask, dmix, zero)
        picks = jnp.where(head_mask((16, width), head), 1.0, 0.0).astype(BF16)
        delta = nt(picks, prod)[0:1, :]
        e = jnp.exp(nt(k, qh) + bias)
        probs = e * (1.0 / jnp.sum(e, 0, keepdims=True))
        dprobs = nt(v, dh)
        ds = (probs * (dprobs - delta)).astype(BF16)
        dv = dv + nn(probs.astype(BF16), dh)
        dk = dk + nn(ds, qh)
        dq = dq + tn(ds, kh)

    def back(low, grad, c):
        full = low.astype(F32)
        sums = head_sums(full * grad, ones)
        t = grad - full * (sums * inv)
        return (c * (t * cosines - partner(t) * sines)).astype(BF16), jnp.sum(sums, 0, keepdims=True)

    gq, sq = back(q, dq, cq_ref[...])
    gk, sk = back(k, dk, ck_ref[...])
    gv = dv.astype(BF16)
    part = nt(gq, w_ref[0]) + nt(gk, w_ref[1]) + nt(gv, w_ref[2])
    at = pl.ds(pl.multiple_of(i * BUCKET, BUCKET), BUCKET)
    tg_ref[0, at, :] = gq
    tg_ref[1, at, :] = gk
    tg_ref[2, at, :] = gv
    mg = tn(mixed, branch)

    @pl.when(i == 0)
    def _():
        scale_ref[...] = sq + sk
        macc_ref[...] = mg

    @pl.when(i > 0)
    def _():
        scale_ref[...] += sq + sk
        macc_ref[...] += mg

    if second:

        @pl.when(i < 2)
        def _():
            keep_ref[...] = part + prev_keep_ref[...]

        @pl.when(i >= 2)
        def _():
            send_ref[...] = (part + prev_send_ref[...]).astype(BF16)
    else:

        @pl.when(i < 2)
        def _():
            keep_ref[...] = part

        @pl.when(i >= 2)
        def _():
            send_ref[...] = part

    @pl.when(i == pl.num_programs(0) - 1)
    def _():
        mgrad_ref[...] = macc_ref[...].astype(BF16)
        for which in range(3):
            hgrad_ref[which] = tn(n_ref[...], tg_ref[which]).astype(BF16)


def attend_backward(
    normed, weight, merge_weight, inv, ones, cosines, sines, valid, branch, saved, prev=None
):
    n, d = normed.shape
    width = weight.shape[2]
    images = n // BUCKET
    heads = width // HEAD_DIM
    half = images // 2
    block = rows(BUCKET, width)
    keep_spec = pl.BlockSpec((BUCKET, d), lambda i: (jnp.minimum(i, half - 1), 0))
    send_spec = pl.BlockSpec((BUCKET, d), lambda i: (jnp.maximum(i - half, 0), 0))
    in_specs = [
        whole(normed.shape),
        whole(weight.shape),
        whole(merge_weight.shape),
        whole(inv.shape),
        whole(ones.shape),
        rows(BUCKET, 128),
        rows(BUCKET, 128),
        pl.BlockSpec((1, BUCKET, 1), lambda i: (i, 0, 0)),
        rows(BUCKET, d),
    ] + [block] * 6
    operands = [
        normed, weight, merge_weight, inv, ones, cosines, sines, valid, branch, *saved,
    ]
    if prev is not None:
        in_specs += [keep_spec, send_spec]
        operands += list(prev)
    return pl.pallas_call(
        functools.partial(attend_backward_kernel, prev is not None, heads),
        grid=(images,),
        in_specs=in_specs,
        out_specs=[
            whole(weight.shape),
            whole(merge_weight.shape),
            whole((1, width)),
            keep_spec,
            send_spec,
        ],
        out_shape=[
            jax.ShapeDtypeStruct(weight.shape, BF16),
            jax.ShapeDtypeStruct(merge_weight.shape, BF16),
            jax.ShapeDtypeStruct((1, width), F32),
            jax.ShapeDtypeStruct((n // 2, d), F32),
            jax.ShapeDtypeStruct((n // 2, d), F32 if prev is None else BF16),
        ],
        scratch_shapes=[
            pltpu.VMEM((3, n, width), BF16),
            pltpu.VMEM(merge_weight.shape, F32),
        ],
        compiler_params=params(),
        cost_estimate=cost(
            2 * (16 * n * d * width + 10 * n * BUCKET * width * heads),
            16 * 1024 * 1024,
            n * BUCKET * heads,
        ),
        name="attend_backward",
    )(*operands)


def geglu_kernel(second, na_ref, nb_ref, ga_ref, gb_ref, e_ref, r_ref, *refs):
    if second:
        prev_ref = refs[0]
        refs = refs[1:]
    o_keep_ref, o_send_ref, n_keep_ref, n_send_ref, grad_ref, ob_ref, nb_acc_ref, act_ref = refs
    j = pl.program_id(0)
    e_gate, e_up, red = e_ref[0], e_ref[1], r_ref[...]
    half = na_ref.shape[0]
    tile = 256
    for t in range(2 * half // tile):
        first = t * tile < half
        at = pl.ds((t * tile) % half, tile)
        normed = (na_ref if first else nb_ref)[at, :]
        g = (ga_ref if first else gb_ref)[at, :]
        gate = nn(normed, e_gate)
        up = nn(normed, e_up)
        hgrad = nt(g, red)
        square = gate * gate
        th = jnp.tanh(gate * (GELU_A + (GELU_A * GELU_B) * square))
        act = 0.5 * (1.0 + th)
        gelu = gate * act
        slope = act + (0.5 * gate) * (1.0 - th * th) * (GELU_A + (3.0 * GELU_A * GELU_B) * square)
        hidden = (gelu * up).astype(BF16)
        d_gate = (hgrad * up * slope).astype(BF16)
        d_up = (hgrad * gelu).astype(BF16)
        whole_at = pl.ds(t * tile, tile)
        act_ref[0, whole_at, :] = hidden
        act_ref[1, whole_at, :] = d_gate
        act_ref[2, whole_at, :] = d_up
        o_part = nn(hidden, red)
        n_part = nt(d_gate, e_gate) + nt(d_up, e_up)
        o_ref = o_keep_ref if first else ob_ref
        n_ref = n_keep_ref if first else nb_acc_ref

        @pl.when(j == 0)
        def _():
            o_ref[at, :] = o_part
            n_ref[at, :] = n_part

        @pl.when(j > 0)
        def _():
            o_ref[at, :] += o_part
            n_ref[at, :] += n_part

    for which in range(3):
        left = ga_ref if which == 0 else na_ref
        right = gb_ref if which == 0 else nb_ref
        total = tn(act_ref[which, :half, :], left[...]) + tn(act_ref[which, half:, :], right[...])
        here = pl.ds(which * CHUNK, CHUNK)
        if second:
            total = total + prev_ref[0, here, :].astype(F32)
        grad_ref[0, here, :] = total.astype(BF16)

    @pl.when(j == pl.num_programs(0) - 1)
    def _():
        o_send_ref[...] = ob_ref[...].astype(BF16)
        n_send_ref[...] = nb_acc_ref[...].astype(BF16)


def geglu(normed_a, normed_b, grad_a, grad_b, expand, reduce, prev=None):
    half, d = normed_a.shape
    units = reduce.shape[0]
    steps = units // CHUNK
    grads = pl.BlockSpec((1, 3 * CHUNK, d), lambda j: (j, 0, 0))
    in_specs = [whole((half, d))] * 4 + [
        pl.BlockSpec((2, d, CHUNK), lambda j: (0, 0, j)),
        pl.BlockSpec((CHUNK, d), lambda j: (j, 0)),
    ]
    operands = [normed_a, normed_b, grad_a, grad_b, expand, reduce]
    if prev is not None:
        in_specs.append(grads)
        operands.append(prev)
    return pl.pallas_call(
        functools.partial(geglu_kernel, prev is not None),
        grid=(steps,),
        in_specs=in_specs,
        out_specs=[whole((half, d))] * 4 + [grads],
        out_shape=[
            jax.ShapeDtypeStruct((half, d), F32),
            jax.ShapeDtypeStruct((half, d), BF16),
            jax.ShapeDtypeStruct((half, d), F32),
            jax.ShapeDtypeStruct((half, d), BF16),
            jax.ShapeDtypeStruct((steps, 3 * CHUNK, d), BF16),
        ],
        scratch_shapes=[
            pltpu.VMEM((half, d), F32),
            pltpu.VMEM((half, d), F32),
            pltpu.VMEM((3, 2 * half, CHUNK), BF16),
        ],
        compiler_params=params(),
        cost_estimate=cost(2 * 9 * 2 * half * d * units, 32 * 1024 * 1024, 2 * half * units),
        name="geglu",
    )(*operands)


def swap(values, axis, size, bit):
    return lax.ppermute(values, axis, [(i, i ^ bit) for i in range(size)])


def reduce_over(values, order, size, index):
    x = values
    for bit in order:
        half = x.shape[0] // 2
        mine = (index & bit) != 0
        low, high = x[:half], x[half:]
        sent = jnp.where(mine, low, high)
        kept = jnp.where(mine, high, low)
        got = swap(sent, "dp", size, bit)
        x = (kept.astype(F32) + got.astype(F32)).astype(BF16)
    for bit in reversed(order):
        mine = (index & bit) != 0
        got = swap(x, "dp", size, bit)
        x = jnp.where(mine, jnp.concatenate([got, x], 0), jnp.concatenate([x, got], 0))
    return x


def rope_tables(bucket_ids):
    quarter = HEAD_DIM // 8
    choose = (bucket_ids[:, None] == jnp.arange(16, dtype=jnp.int32)[None, :]).astype(jnp.int32)
    heights = jnp.sum(choose * jnp.asarray(GRID_ROWS)[None, :], axis=1)
    widths = jnp.sum(choose * jnp.asarray(GRID_COLS)[None, :], axis=1)
    places = jnp.arange(BUCKET, dtype=jnp.int32)[None, :]
    row_pos = (places // widths[:, None]).reshape(-1)
    col_pos = (places % widths[:, None]).reshape(-1)
    valid = places < (heights * widths)[:, None]
    lane = np.arange(128) % HEAD_DIM
    freqs = 10000.0 ** (-jnp.arange(quarter, dtype=F32) / quarter)
    freqs = freqs[lane % quarter]
    by_row = jnp.asarray((lane // quarter) % 2 == 0)
    turns = jnp.asarray(lane < HEAD_DIM // 2)
    sign = jnp.asarray(np.where(lane < HEAD_DIM // 4, -1.0, 1.0).astype(np.float32))
    where = jnp.where(by_row[None, :], row_pos[:, None], col_pos[:, None]).astype(F32)
    angles = where * freqs[None, :]
    cosines = jnp.where(turns[None, :], jnp.cos(angles), 1.0)
    sines = jnp.where(turns[None, :], jnp.sin(angles) * sign[None, :], 0.0)
    bias = jnp.where(valid, 0.0, NEG).astype(F32)
    return cosines, sines, bias


def per_device(
    dp,
    mp,
    tokens,
    condition,
    buckets,
    heads_weight,
    merge_weight,
    expand_weight,
    reduce_weight,
    adapt_first,
    adapt_second,
    cosine_scale,
    cotangent,
):
    own_rows, width = tokens.shape
    local_images = buckets.shape[0]
    local_heads = cosine_scale.shape[0]
    local = local_heads * HEAD_DIM
    units = reduce_weight.shape[0]
    index = lax.axis_index("dp")
    core = functools.partial(swap, axis="mp", size=mp, bit=1)
    chip = functools.partial(swap, axis="mp", size=mp, bit=2)

    heads_own = jnp.transpose(heads_weight, (1, 0, 2))
    heads_other = chip(heads_own)
    merge_other = chip(merge_weight)
    scale_other = chip(cosine_scale)
    cot_chip = chip(cotangent)
    cot_core = core(cotangent)
    cot_far = core(cot_chip)

    scale_first = 1.0 + jnp.dot(condition, adapt_first, preferred_element_type=F32)
    scale_second = 1.0 + jnp.dot(condition, adapt_second, preferred_element_type=F32)
    scale_first = scale_first.reshape(local_images, 1, width)
    scale_second = scale_second.reshape(local_images, 1, width)
    normed_own = norm_first(tokens, scale_first)
    normed = jnp.concatenate([normed_own, core(normed_own)], 0)
    cosines, sines, bias = rope_tables(jnp.concatenate([buckets, core(buckets)], 0))
    bias_row = bias[:, None, :]
    bias_column = bias[:, :, None]
    expand_own = jnp.transpose(expand_weight, (1, 0, 2))
    head_of = np.arange(local) // HEAD_DIM
    ones = jnp.asarray((head_of[:, None] == head_of[None, :]).astype(np.float32)).astype(BF16)

    def lanes(values):
        return jnp.repeat(values, HEAD_DIM)[None, :]

    own = attend_forward(
        normed, heads_own, lanes(jnp.sqrt(cosine_scale)), ones, cosines, sines, bias_row
    )
    *other, keep, send = attend_forward(
        normed,
        heads_other,
        lanes(jnp.sqrt(scale_other)),
        ones,
        cosines,
        sines,
        bias_row,
        (own[5], merge_weight, merge_other),
    )
    middle, second_own = norm_second(tokens, keep, core(send), scale_second)
    second_chip = chip(second_own)
    second_core = core(second_own)
    second_far = core(second_chip)

    o_keep, o_send, n_keep, n_send, grads = geglu(
        second_own, second_core, cotangent, cot_core, expand_own, reduce_weight
    )
    o_chip, o_far, n_chip, n_far, grads = geglu(
        second_chip, second_far, cot_chip, cot_far, expand_own, reduce_weight, grads
    )

    n_sum = chip((n_chip + core(n_far).astype(F32)).astype(BF16))
    n_near = core(n_send)
    middle_grad, adapt_second_grad, branch_own = norm_back(
        n_keep, (n_near, n_sum), middle, cotangent, scale_second, True
    )
    o_sum = chip((o_chip + core(o_far).astype(F32)).astype(BF16))
    layer_out = middle + (o_keep + core(o_send).astype(F32) + o_sum.astype(F32))

    branch = jnp.concatenate([branch_own, core(branch_own)], 0)
    heads_far, merge_far, turn_far, keep, send = attend_backward(
        normed,
        heads_other,
        merge_other,
        lanes(1.0 / scale_other),
        ones,
        cosines,
        sines,
        bias_column,
        branch,
        other,
    )
    heads_got, merge_got = chip(heads_far), chip(merge_far)
    heads_near, merge_near, turn_own, keep, send = attend_backward(
        normed,
        heads_own,
        merge_weight,
        lanes(1.0 / cosine_scale),
        ones,
        cosines,
        sines,
        bias_column,
        branch,
        own,
        (keep, send),
    )
    tokens_grad, adapt_first_grad = norm_back(
        keep, (core(send),), tokens, middle_grad, scale_first, False
    )

    bits = [1 << b for b in range(dp.bit_length() - 1)]
    turned = bits[1:2] + bits[:1] + bits[2:]
    blocks = [
        reduce_over(grads[j], turned if j == 2 else bits, dp, index) for j in range(grads.shape[0])
    ]
    merge_sum = reduce_over(
        (merge_near.astype(F32) + merge_got.astype(F32)).astype(BF16), turned, dp, index
    )
    heads_sum = [
        reduce_over(
            (heads_near[c].astype(F32) + heads_got[c].astype(F32)).astype(BF16), bits, dp, index
        )
        for c in range(3)
    ]
    blocks = jnp.stack(blocks).astype(F32).reshape(-1, 3, CHUNK, width)
    reduce_total = blocks[:, 0].reshape(units, width)
    expand_total = jnp.transpose(blocks[:, 1:], (3, 1, 0, 2)).reshape(width, 2, units)
    heads_total = jnp.transpose(jnp.stack(heads_sum).astype(F32), (1, 0, 2))
    merge_total = merge_sum.astype(F32)

    first_low = adapt_first_grad.reshape(local_images, width).astype(BF16)
    second_low = adapt_second_grad.reshape(local_images, width).astype(BF16)
    condition_grad = nt(first_low, adapt_first) + nt(second_low, adapt_second)
    pad = ((0, 0), (0, width - condition.shape[1]))
    turn_far_got = chip(turn_far)
    turn = jnp.pad(turn_own + turn_far_got, ((0, 0), (0, width - local)))
    payload = jnp.concatenate(
        [
            first_low.astype(F32),
            second_low.astype(F32),
            jnp.pad(condition.astype(F32), pad),
            turn,
            jnp.zeros((1, width), F32),
        ],
        0,
    )[None]
    for bit in bits:
        payload = jnp.concatenate([payload, swap(payload, "dp", dp, bit)], 0)
    turn_total = jnp.sum(payload[:, 3 * local_images, :local], 0)
    for bit in (1, 2):
        payload = jnp.concatenate([payload, swap(payload, "mp", mp, bit)], 0)
    n = local_images
    first_all = payload[:, :n].reshape(-1, width).astype(BF16)
    second_all = payload[:, n : 2 * n].reshape(-1, width).astype(BF16)
    condition_all = payload[:, 2 * n : 3 * n, : condition.shape[1]]
    condition_all = condition_all.reshape(-1, condition.shape[1]).astype(BF16)
    first_total = tn(condition_all, first_all)
    second_total = tn(condition_all, second_all)
    scale_total = turn_total[::HEAD_DIM] / (2.0 * cosine_scale)
    return (
        layer_out,
        tokens_grad,
        condition_grad,
        heads_total,
        merge_total,
        expand_total,
        reduce_total,
        first_total,
        second_total,
        scale_total,
    )


def solution(mesh):
    split = P(("dp", "mp"), None)
    return jax.shard_map(
        functools.partial(per_device, mesh.shape["dp"], mesh.shape["mp"]),
        mesh=mesh,
        in_specs=(
            split,
            split,
            P(("dp", "mp")),
            P(None, None, "mp"),
            P("mp", None),
            P(None, None, "mp"),
            P("mp", None),
            P(),
            P(),
            P("mp"),
            split,
        ),
        out_specs=(
            split,
            split,
            split,
            P(None, None, "mp"),
            P("mp", None),
            P(None, None, "mp"),
            P("mp", None),
            P(),
            P(),
            P("mp"),
        ),
        check_vma=False,
    )
```

time: 1190 us -> 502 us (0.42)
  waiting for transfers between devices: 893 us -> 187 us
  Pallas kernels: 0 us -> 136 us
  matrix products: 137 us -> 9.34 us
  starting transfers between devices: 1.14 us -> 74 us
  local copies, waits for them, and re-layouts: 73 us -> 30.7 us
  blocking collectives: 28.5 us -> 0 us
  other arithmetic: 36.1 us -> 57.5 us
  between operations: 15.9 us -> 2.09 us
    psum x2 -> x0, waiting for transfers between devices: 575 us -> none  [the longest x1 426 us: per_device(): lax.psum((heads_local, merge_local, expand_local, reduce_local, scale_loc...]
    reduce_scatter x4 -> x0, waiting for transfers between devices: 205 us -> none  [the longest x1 71.8 us: per_device(): lax.psum_scatter(lax.dot_general(gate_up_low, expand_flat, contract_last,...]
    ppermute x0 -> x70, waiting for transfers between devices: none -> 187 us  [swap(): return lax.ppermute(values, axis, [(i, i ^ bit) for i in range(size)])]
    pallas_call x0 -> x10, Pallas kernels: none -> 136 us  [the longest x2 56.3 us: geglu(): pl.pallas_call(functools.partial(geglu_kernel, prev is not None), grid=(s...]
    dot_general x23 -> x6, matrix products: 129 us -> 9.34 us  [the longest x2 6.42 us: tn(): lax.dot_general(a, b, (((0,), (0,)), ((), ())), preferred_element_type=F32)]
    all_gather x4 -> x0, waiting for transfers between devices: 113 us -> none  [the longest x1 34.4 us: per_device(): attend_group = lax.all_gather(attend_low, 'mp', axis=0, tiled=True)]
    ppermute x0 -> x70, starting transfers between devices: none -> 74 us  [swap(): return lax.ppermute(values, axis, [(i, i ^ bit) for i in range(size)])]
    unnamed x125 -> x73, local copies, waits for them, and re-layouts: 44.4 us -> 17.5 us
  transfers between devices with their start and end apart: 10 -> 70, of which waited for: 9 -> 36; matrix products, arithmetic and copies ran while one was open for 9% -> 17% of each run, Pallas kernels for 0% -> 18%
where the time goes in v1:
time: 502 us; the launch traced here: 496 us
  waiting for transfers between devices  187 us (37%)
  Pallas kernels  136 us (27%)
  starting transfers between devices  74 us (15%)
  other arithmetic  57.5 us (11%)
  local copies, waits for them, and re-layouts  30.7 us (6%)
  matrix products  9.34 us (2%)
    ppermute x70, waiting for transfers between devices, swap(): return lax.ppermute(values, axis, [(i, i ^ bit) for i in range(size)])  187 us
    ppermute x70, starting transfers between devices, swap(): return lax.ppermute(values, axis, [(i, i ^ bit) for i in range(size)])  74 us
    pallas_call x2, Pallas kernels, geglu(): pl.pallas_call(functools.partial(geglu_kernel, prev is not None), grid=(s...  56.3 us
    pallas_call x2, Pallas kernels, attend_backward(): pl.pallas_call(functools.partial(attend_backward_kernel, prev is not None...  40.9 us
    pallas_call x2, Pallas kernels, attend_forward(): pl.pallas_call(functools.partial(attend_forward_kernel, merge is not None...  23.4 us
    unnamed x73, local copies, waits for them, and re-layouts  17.5 us
    select_n x23, other arithmetic, reduce_over(): jnp.where(mine, jnp.concatenate([got, x], 0), jnp.concatenate([x, got], 0))  13.1 us
  transfers between devices with their start and end apart: 70, of which 36 were waited for; matrix products, arithmetic and copies ran while one was open for 17% of the time, Pallas kernels for 18%

profile of v1, /device:TPU:0, one launch (start us, length us, event | category | flops | bytes accessed | tf_op | source)
XLA Modules:
  0.0 495.9 jit_solution(14166218440666938931)
XLA Ops:
  3.7 2.3 norm_first.1
  6.4 2.6 collective-permute-start.1
  9.2 1.8 collective-permute-start.4
  12.4 5.2 %select_select_fusion = f32[128]{0:T(128)S(1)} fusion(pred[128]{0:T(512)(128)(4,1)S(1)} %copy-done.20, pred[128]{0:T(512)(128)(4,1)S(1)} %copy-done.21, pred[128]{0:T(512)(128)(4,1)S(1)} %copy-done.22, pred[128]{0:T(512)(128)(4,1)S(1)} %copy-done.23, pred[128]{0:T(512)(128)(4,1)S(1)} %copy-done.24, pred[128]{0:T(512)(128)(4,1)S(1)} %copy-done.25, ...), kind=kLoop, calls=%fused_computation.127 | loop fusion | flops 896 | bytes 1440 | tf_op jit(solution)/shard_map/gather | solution.py:546
  19.1 3.1 multiply_select_fusion
  22.2 22.3 %collective-permute-done.2 = f32[4]{0:T(128)S(1)} collective-permute-done((f32[4]{0:T(128)S(1)}, f32[4]{0:T(128)S(1)}, u32[]{:S(2)}, u32[]{:S(2)}) %collective-permute-start.2) | collective-permute-done | bytes 48 | tf_op jit(solution)/shard_map/ppermute | solution.py:515
  45.3 2.7 pad_maximum_fusion.n_ref
  48.0 10.2 %attend_forward.2 = (bf16[1024,256]{1,0:T(8,128)(2,1)}, bf16[1024,256]{1,0:T(8,128)(2,1)}, bf16[1024,256]{1,0:T(8,128)(2,1)}, f32[1024,256]{1,0:T(8,128)}, f32[1...) custom-call(bf16[1024,1024]{1,0:T(8,128)(2,1)} %pad_maximum_fusion.n_ref, bf16[3,1024,256]{2,1,0:T(8,128)(2,1)} %bitcast.w_ref, ...), custom_call_target="tpu_custom_call" | custom-call | flops 5368709120 | bytes 12582912 | tf_op jit(solution)/shard_map/attend_forward/pallas_call | solution.py:241
  58.2 13.2 %attend_forward.3 = (bf16[1024,256]{1,0:T(8,128)(2,1)}, bf16[1024,256]{1,0:T(8,128)(2,1)}, bf16[1024,256]{1,0:T(8,128)(2,1)}, f32[1024,256]{1,0:T(8,128)}, f32[1...) custom-call(bf16[1024,1024]{1,0:T(8,128)(2,1)} %pad_maximum_fusion.n_ref, ...), custom_call_target="tpu_custom_call" | custom-call | flops 7516192768 | bytes 12582912 | tf_op jit(solution)/shard_map/attend_forward/pallas_call | solution.py:241
  71.5 2.0 collective-permute-start.11
  75.4 3.6 norm_second.1
  79.1 1.9 collective-permute-start.9
  81.4 2.1 copy.79
  83.5 14.4 %collective-permute-done.11.ga_ref = bf16[512,1024]{1,0:T(8,128)(2,1)} collective-permute-done((bf16[512,1024]{1,0:T(8,128)(2,1)}, bf16[512,1024]{1,0:T(8,128)(2,1)}, u32[]{:S(2)}, u32[]{:S(2)}) %collective-permute-start.11) | collective-permute-done | bytes 1048608 | tf_op jit(solution)/shard_map/ppermute | solution.py:515
  97.9 22.1 %collective-permute-done.9.na_ref = bf16[512,1024]{1,0:T(8,128)(2,1)} collective-permute-done((bf16[512,1024]{1,0:T(8,128)(2,1)}, bf16[512,1024]{1,0:T(8,128)(2,1)}, u32[]{:S(2)}, u32[]{:S(2)}) %collective-permute-start.9) | collective-permute-done | bytes 1048608 | tf_op jit(solution)/shard_map/ppermute | solution.py:515
  120.1 27.6 %geglu.2 = (f32[512,1024]{1,0:T(8,128)}, bf16[512,1024]{1,0:T(8,128)(2,1)}, f32[512,1024]{1,0:T(8,128)}, bf16[512,1024]{1,0:T(8,128)(2,1)}, bf16[3,768,1024]{2,1,0:T(8,128)(2,1)}) custom-call(bf16[512,1024]{1,0:T(8,128)(2,1)} %get-tuple-element.55.na_ref, bf16[512,1024]{1,0:T(8,128)(2,1)} %collective-permute-done.6.nb_ref, bf16[512,1024]{1,0:T(8,128)(2,1)} %refs_4_.1, ...), custom_call_target="tpu_custom_call" | custom-call | flops 14495514624 | bytes 33554432 | tf_op jit(solution)/shard_map/geglu/pallas_call | solution.py:491
  149.0 28.6 %geglu.3 = (f32[512,1024]{1,0:T(8,128)}, bf16[512,1024]{1,0:T(8,128)(2,1)}, f32[512,1024]{1,0:T(8,128)}, bf16[512,1024]{1,0:T(8,128)(2,1)}, bf16[3,768,1024]{2,1,0:T(8,128)(2,1)}) custom-call(bf16[512,1024]{1,0:T(8,128)(2,1)} %collective-permute-done.9.na_ref, bf16[512,1024]{1,0:T(8,128)(2,1)} %copy-done.28, ...), custom_call_target="tpu_custom_call" | custom-call | flops 14495514624 | bytes 33554432 | tf_op jit(solution)/shard_map/geglu/pallas_call | solution.py:491
  177.7 3.8 select_bitcast_fusion.2
  188.2 13.9 %collective-permute-done.46 = bf16[384,1024]{1,0:T(8,128)(2,1)} collective-permute-done((bf16[384,1024]{1,0:T(8,128)(2,1)}, bf16[384,1024]{1,0:T(8,128)(2,1)}, u32[]{:S(2)}, u32[]{:S(2)}) %collective-permute-start.46) | collective-permute-done | bytes 786464 | tf_op jit(solution)/shard_map/ppermute | solution.py:515
  203.2 15.4 %collective-permute-done.52 = bf16[384,1024]{1,0:T(8,128)(2,1)} collective-permute-done((bf16[384,1024]{1,0:T(8,128)(2,1)}, bf16[384,1024]{1,0:T(8,128)(2,1)}, u32[]{:S(2)}, u32[]{:S(2)}) %collective-permute-start.52) | collective-permute-done | bytes 786464 | tf_op jit(solution)/shard_map/ppermute | solution.py:515
  218.6 4.7 fusion.2
  223.4 1.8 collective-permute-start.59
  227.8 6.3 %collective-permute-done.59 = bf16[192,1024]{1,0:T(8,128)(2,1)S(1)} collective-permute-done((bf16[192,1024]{1,0:T(8,128)(2,1)S(1)}, bf16[192,1024]{1,0:T(8,128)(2,1)S(1)}, u32[]{:S(2)}, u32[]{:S(2)}) %collective-permute-start.59) | collective-permute-done | bytes 393248 | tf_op jit(solution)/shard_map/ppermute | solution.py:515
  237.3 2.6 collective-permute-start.60
  240.2 8.2 %collective-permute-done.47 = bf16[192,1024]{1,0:T(8,128)(2,1)S(1)} collective-permute-done((bf16[192,1024]{1,0:T(8,128)(2,1)S(1)}, bf16[192,1024]{1,0:T(8,128)(2,1)S(1)}, u32[]{:S(2)}, u32[]{:S(2)}) %collective-permute-start.47) | collective-permute-done | bytes 393248 | tf_op jit(solution)/shard_map/ppermute | solution.py:515
  251.7 12.5 %collective-permute-done.54 = bf16[96,1024]{1,0:T(8,128)(2,1)S(1)} collective-permute-done((bf16[96,1024]{1,0:T(8,128)(2,1)S(1)}, bf16[96,1024]{1,0:T(8,128)(2,1)S(1)}, u32[]{:S(2)}, u32[]{:S(2)}) %collective-permute-start.54) | collective-permute-done | bytes 196640 | tf_op jit(solution)/shard_map/ppermute | solution.py:515
  264.3 8.3 %collective-permute-done.48 = bf16[96,1024]{1,0:T(8,128)(2,1)S(1)} collective-permute-done((bf16[96,1024]{1,0:T(8,128)(2,1)S(1)}, bf16[96,1024]{1,0:T(8,128)(2,1)S(1)}, u32[]{:S(2)}, u32[]{:S(2)}) %collective-permute-start.48) | collective-permute-done | bytes 196640 | tf_op jit(solution)/shard_map/ppermute | solution.py:515
  272.8 4.1 collective-permute-done.61
  277.0 8.6 %collective-permute-done.55 = bf16[96,1024]{1,0:T(8,128)(2,1)S(1)} collective-permute-done((bf16[96,1024]{1,0:T(8,128)(2,1)S(1)}, bf16[96,1024]{1,0:T(8,128)(2,1)S(1)}, u32[]{:S(2)}, u32[]{:S(2)}) %collective-permute-start.55) | collective-permute-done | bytes 196640 | tf_op jit(solution)/shard_map/ppermute | solution.py:515
  286.2 2.6 collective-permute-start.56
  290.2 2.5 collective-permute-done.49
  295.8 2.7 collective-permute-done.56
  298.5 2.5 collective-permute-start.50
  302.6 4.8 norm_back.2
  308.6 2.5 collective-permute-done.50
  315.7 2.9 collective-permute-done.14
  318.6 3.5 add_add_fusion
  322.1 4.0 collective-permute-done.63
  326.1 2.1 maximum_select_fusion.2
  329.6 20.0 %attend_backward.2 = (bf16[3,1024,256]{2,1,0:T(8,128)(2,1)}, bf16[256,1024]{1,0:T(8,128)(2,1)}, f32[1,256]{1,0:T(1,128)}, f32[512,1024]{1,0:T(8,128)}, f32[512,1024]{1,0:T(8,128)}) custom-call(bf16[1024,1024]{1,0:T(8,128)(2,1)} %pad_maximum_fusion.n_ref, bf16[3,1024,256]{2,1,0:T(8,128)(2,1)} %collective-permute-done.1.w_ref, ...), custom_call_target="tpu_custom_call" | custom-call | flops 13958643712 | bytes 16777216 | tf_op jit(solution)/shard_map/attend_backward/pallas_call | solution.py:387
  350.7 20.9 %attend_backward.3 = (bf16[3,1024,256]{2,1,0:T(8,128)(2,1)}, bf16[256,1024]{1,0:T(8,128)(2,1)}, f32[1,256]{1,0:T(1,128)}, f32[512,1024]{1,0:T(8,128)}, bf16[512,1024]{1,0:T(8,128)(2,1)}) custom-call(bf16[1024,1024]{1,0:T(8,128)(2,1)} %pad_maximum_fusion.n_ref, bf16[3,1024,256]{2,1,0:T(8,128)(2,1)} %bitcast.w_ref, bf16[256,1024]{1,0:T(8,128)(2,1)} %m_ref.1, ...), custom_call_target="tpu_custom_call" | custom-call | flops 13958643712 | bytes 16777216 | tf_op jit(solution)/shard_map/attend_backward/pallas_call | solution.py:387
  374.4 2.1 maximum_select_fusion.1
  376.6 2.1 maximum_select_fusion
  382.4 2.5 collective-permute-done.41
  384.9 5.4 %collective-permute-start.42 = (bf16[32,1024]{1,0:T(8,128)(2,1)S(1)}, bf16[32,1024]{1,0:T(8,128)(2,1)S(1)}, u32[]{:S(2)}, u32[]{:S(2)}) collective-permute-start(bf16[32,1024]{1,0:T(8,128)(2,1)S(1)} %broadcast_select_fusion.11), channel_id=1, source_target_pairs={{0,16},{4,20},{8,24},{12,28},{16,0},{20,4},{24,8},{28,12},{1,17},{... | collective-permute-start | bytes 196616 | tf_op jit(solution)/shard_map/ppermute | solution.py:515
  390.4 1.9 maximum_convert_fusion.1
  392.3 3.2 slice.292
  395.4 10.2 %copy.62 = f32[1024,2,768]{2,1,0:T(2,128)} copy(f32[1024,2,768]{0,2,1:T(8,128)} %bitcast.101) | data formatting | bytes 12582912
  406.2 4.3 norm_back.3
  411.9 3.5 collective-permute-done.65
  416.9 3.0 collective-permute-done.66
  420.0 3.5 collective-permute-start.67
  433.7 9.2 %collective-permute-done.20 = bf16[3,1024,256]{2,1,0:T(8,128)(2,1)} collective-permute-done((bf16[3,1024,256]{2,1,0:T(8,128)(2,1)}, bf16[3,1024,256]{2,1,0:T(8,128)(2,1)}, u32[]{:S(2)}, u32[]{:S(2)}) %collective-permute-start.20) | collective-permute-done | bytes 1572896 | tf_op jit(solution)/shard_map/ppermute | solution.py:515
  442.9 2.2 add_convert_fusion.5
  449.6 3.4 concatenate.439
  453.0 3.2 convolution_bitcast_fusion.1
  458.8 1.8 collective-permute-start.28
  469.9 2.1 collective-permute-start.36
  478.7 1.9 collective-permute-start.25
  481.2 1.9 collective-permute-start.38
  483.2 1.9 collective-permute-start.32
  486.5 3.2 convolution_bitcast_fusion
  490.7 2.6 collective-permute-done.26
  493.5 1.9 convert_bitcast_fusion
  (283 shorter events, 89.5 us)
Async XLA Ops:
  5.9 39.3 %collective-permute-start = (bf16[512,1024]{1,0:T(8,128)(2,1)}, bf16[512,1024]{1,0:T(8,128)(2,1)}, u32[]{:S(2)}, u32[]{:S(2)}) collective-permute-start(bf16[512,1024]{1,0:T(8,128)(2,1)} %norm_first.1), channel_id=1, source_target_pairs={{0,1},{1,0},{2,3},{3,2},{4,5},{5,4},{6,7},{7,6},{8,9},{9,8},{10,11... | collective-permute-start | bytes 3145736 | tf_op jit(solution)/shard_map/ppermute | solution.py:515
  6.4 51.8 %collective-permute-start.1 = (bf16[3,1024,256]{2,1,0:T(8,128)(2,1)}, bf16[3,1024,256]{2,1,0:T(8,128)(2,1)}, u32[]{:S(2)}, u32[]{:S(2)}) collective-permute-start(bf16[3,1024,256]{2,1,0:T(8,128)(2,1)} %bitcast.w_ref), channel_id=1, source_target_pairs={{0,2},{1,3},{2,0},{3,1},{4,6},{5,7},{6,4},{7,5},{8,10},{9,11},{10,... | collective-permute-start | bytes 4718600 | tf_op jit(solution)/shard_map/ppermute | solution.py:515
  9.0 35.6 %collective-permute-start.2 = (f32[4]{0:T(128)S(1)}, f32[4]{0:T(128)S(1)}, u32[]{:S(2)}, u32[]{:S(2)}) collective-permute-start(f32[4]{0:T(128)S(1)} %copy-done.31), channel_id=1, source_target_pairs={{0,2},{1,3},{2,0},{3,1},{4,6},{5,7},{6,4},{7,5},{8,10},{9,11},{10,... | collective-permute-start | bytes 56 | tf_op jit(solution)/shard_map/ppermute | solution.py:515
  9.1 8.5 %collective-permute-start.3 = (s32[2]{0:T(128)S(1)}, s32[2]{0:T(128)S(1)}, u32[]{:S(2)}, u32[]{:S(2)}) collective-permute-start(s32[2]{0:T(128)S(1)} %copy-done.30), channel_id=1, source_target_pairs={{0,1},{1,0},{2,3},{3,2},{4,5},{5,4},{6,7},{7,6},{8,9},{9,8},{10,11... | collective-permute-start | bytes 32 | tf_op jit(solution)/shard_map/ppermute | solution.py:515
  9.2 49.0 %collective-permute-start.4 = (bf16[256,1024]{1,0:T(8,128)(2,1)}, bf16[256,1024]{1,0:T(8,128)(2,1)}, u32[]{:S(2)}, u32[]{:S(2)}) collective-permute-start(bf16[256,1024]{1,0:T(8,128)(2,1)} %m_ref.1), channel_id=1, source_target_pairs={{0,2},{1,3},{2,0},{3,1},{4,6},{5,7},{6,4},{7,5},{8,10},{9,11},{10,... | collective-permute-start | bytes 1572872 | tf_op jit(solution)/shard_map/ppermute | solution.py:515
  71.5 26.4 %collective-permute-start.11 = (bf16[512,1024]{1,0:T(8,128)(2,1)}, bf16[512,1024]{1,0:T(8,128)(2,1)}, u32[]{:S(2)}, u32[]{:S(2)}) collective-permute-start(bf16[512,1024]{1,0:T(8,128)(2,1)} %refs_4_.1), channel_id=1, source_target_pairs={{0,2},{1,3},{2,0},{3,1},{4,6},{5,7},{6,4},{7,5},{8,10},{9,11},{10,... | collective-permute-start | bytes 3145736 | tf_op jit(solution)/shard_map/ppermute | solution.py:515
  79.1 41.0 %collective-permute-start.9 = (bf16[512,1024]{1,0:T(8,128)(2,1)}, bf16[512,1024]{1,0:T(8,128)(2,1)}, u32[]{:S(2)}, u32[]{:S(2)}) collective-permute-start(bf16[512,1024]{1,0:T(8,128)(2,1)} %get-tuple-element.55.na_ref), channel_id=1, source_target_pairs={{0,2},{1,3},{2,0},{3,1},{4,6},{5,7},{6,4},{7,5},{8,10},{9,11},{10,... | collective-permute-start | bytes 3145736 | tf_op jit(solution)/shard_map/ppermute | solution.py:515
  80.9 39.1 %collective-permute-start.7 = (bf16[512,1024]{1,0:T(8,128)(2,1)}, bf16[512,1024]{1,0:T(8,128)(2,1)}, u32[]{:S(2)}, u32[]{:S(2)}) collective-permute-start(bf16[512,1024]{1,0:T(8,128)(2,1)} %refs_4_.1), channel_id=1, source_target_pairs={{0,1},{1,0},{2,3},{3,2},{4,5},{5,4},{6,7},{7,6},{8,9},{9,8},{10,11... | collective-permute-start | bytes 3145736 | tf_op jit(solution)/shard_map/ppermute | solution.py:515
  80.9 39.1 %collective-permute-start.6 = (bf16[512,1024]{1,0:T(8,128)(2,1)}, bf16[512,1024]{1,0:T(8,128)(2,1)}, u32[]{:S(2)}, u32[]{:S(2)}) collective-permute-start(bf16[512,1024]{1,0:T(8,128)(2,1)} %get-tuple-element.55.na_ref), channel_id=1, source_target_pairs={{0,1},{1,0},{2,3},{3,2},{4,5},{5,4},{6,7},{7,6},{8,9},{9,8},{10,11... | collective-permute-start | bytes 3145736 | tf_op jit(solution)/shard_map/ppermute | solution.py:515
  97.9 49.8 %collective-permute-start.12 = (bf16[512,1024]{1,0:T(8,128)(2,1)}, bf16[512,1024]{1,0:T(8,128)(2,1)S(1)}, u32[]{:S(2)}, u32[]{:S(2)}) collective-permute-start(bf16[512,1024]{1,0:T(8,128)(2,1)} %collective-permute-done.11.ga_ref), channel_id=1, source_target_pairs={{0,1},{1,0},{2,3},{3,2},{4,5},{5,4},{6,7},{7,6},{8,9},{9,8},{10,11... | collective-permute-start | bytes 3145736 | tf_op jit(solution)/shard_map/ppermute | solution.py:515
  120.0 27.7 %collective-permute-start.10 = (bf16[512,1024]{1,0:T(8,128)(2,1)}, bf16[512,1024]{1,0:T(8,128)(2,1)S(1)}, u32[]{:S(2)}, u32[]{:S(2)}) collective-permute-start(bf16[512,1024]{1,0:T(8,128)(2,1)} %collective-permute-done.9.na_ref), channel_id=1, source_target_pairs={{0,1},{1,0},{2,3},{3,2},{4,5},{5,4},{6,7},{7,6},{8,9},{9,8},{10,11... | collective-permute-start | bytes 3145736 | tf_op jit(solution)/shard_map/ppermute | solution.py:515
  181.5 20.7 %collective-permute-start.46 = (bf16[384,1024]{1,0:T(8,128)(2,1)}, bf16[384,1024]{1,0:T(8,128)(2,1)}, u32[]{:S(2)}, u32[]{:S(2)}) collective-permute-start(bf16[384,1024]{1,0:T(8,128)(2,1)} %get-tuple-element.129), channel_id=1, source_target_pairs={{0,4},{4,0},{8,12},{12,8},{16,20},{20,16},{24,28},{28,24},{1,5},{5... | collective-permute-start | bytes 2359304 | tf_op jit(solution)/shard_map/ppermute | solution.py:515
  183.2 20.0 %collective-permute-start.58 = (bf16[384,1024]{1,0:T(8,128)(2,1)}, bf16[384,1024]{1,0:T(8,128)(2,1)}, u32[]{:S(2)}, u32[]{:S(2)}) collective-permute-start(bf16[384,1024]{1,0:T(8,128)(2,1)} %get-tuple-element.130), channel_id=1, source_target_pairs={{0,8},{4,12},{8,0},{12,4},{16,24},{20,28},{24,16},{28,20},{1,9},{5... | collective-permute-start | bytes 2359304 | tf_op jit(solution)/shard_map/ppermute | solution.py:515
  184.8 33.8 %collective-permute-start.52 = (bf16[384,1024]{1,0:T(8,128)(2,1)}, bf16[384,1024]{1,0:T(8,128)(2,1)}, u32[]{:S(2)}, u32[]{:S(2)}) collective-permute-start(bf16[384,1024]{1,0:T(8,128)(2,1)} %get-tuple-element.131), channel_id=1, source_target_pairs={{0,4},{4,0},{8,12},{12,8},{16,20},{20,16},{24,28},{28,24},{1,5},{5... | collective-permute-start | bytes 2359304 | tf_op jit(solution)/shard_map/ppermute | solution.py:515
  187.7 114.9 %collective-permute-start.15 = (bf16[512,1024]{1,0:T(8,128)(2,1)}, bf16[512,1024]{1,0:T(8,128)(2,1)}, u32[]{:S(2)}, u32[]{:S(2)}) collective-permute-start(bf16[512,1024]{1,0:T(8,128)(2,1)} %get-tuple-element.62), channel_id=1, source_target_pairs={{0,1},{1,0},{2,3},{3,2},{4,5},{5,4},{6,7},{7,6},{8,9},{9,8},{10,11... | collective-permute-start | bytes 3145736 | tf_op jit(solution)/shard_map/ppermute | solution.py:515
  187.7 98.5 %collective-permute-start.13 = (bf16[512,1024]{1,0:T(8,128)(2,1)}, bf16[512,1024]{1,0:T(8,128)(2,1)S(1)}, u32[]{:S(2)}, u32[]{:S(2)}) collective-permute-start(bf16[512,1024]{1,0:T(8,128)(2,1)} %get-tuple-element.60), channel_id=1, source_target_pairs={{0,1},{1,0},{2,3},{3,2},{4,5},{5,4},{6,7},{7,6},{8,9},{9,8},{10,11... | collective-permute-start | bytes 3145736 | tf_op jit(solution)/shard_map/ppermute | solution.py:515
  202.2 24.7 %collective-permute-start.16 = (bf16[512,1024]{1,0:T(8,128)(2,1)}, bf16[512,1024]{1,0:T(8,128)(2,1)S(1)}, u32[]{:S(2)}, u32[]{:S(2)}) collective-permute-start(bf16[512,1024]{1,0:T(8,128)(2,1)} %get-tuple-element.64), channel_id=1, source_target_pairs={{0,1},{1,0},{2,3},{3,2},{4,5},{5,4},{6,7},{7,6},{8,9},{9,8},{10,11... | collective-permute-start | bytes 3145736 | tf_op jit(solution)/shard_map/ppermute | solution.py:515
  223.4 10.8 %collective-permute-start.59 = (bf16[192,1024]{1,0:T(8,128)(2,1)S(1)}, bf16[192,1024]{1,0:T(8,128)(2,1)S(1)}, u32[]{:S(2)}, u32[]{:S(2)}) collective-permute-start(bf16[192,1024]{1,0:T(8,128)(2,1)S(1)} %broadcast_select_fusion), channel_id=1, source_target_pairs={{0,4},{4,0},{8,12},{12,8},{16,20},{20,16},{24,28},{28,24},{1,5},{5... | collective-permute-start | bytes 1179656 | tf_op jit(solution)/shard_map/ppermute | solution.py:515
  225.2 12.1 %collective-permute-start.53 = (bf16[192,1024]{1,0:T(8,128)(2,1)S(1)}, bf16[192,1024]{1,0:T(8,128)(2,1)S(1)}, u32[]{:S(2)}, u32[]{:S(2)}) collective-permute-start(bf16[192,1024]{1,0:T(8,128)(2,1)S(1)} %broadcast_select_fusion.1), channel_id=1, source_target_pairs={{0,8},{4,12},{8,0},{12,4},{16,24},{20,28},{24,16},{28,20},{1,9},{5... | collective-permute-start | bytes 1179656 | tf_op jit(solution)/shard_map/ppermute | solution.py:515
  226.9 21.5 %collective-permute-start.47 = (bf16[192,1024]{1,0:T(8,128)(2,1)S(1)}, bf16[192,1024]{1,0:T(8,128)(2,1)S(1)}, u32[]{:S(2)}, u32[]{:S(2)}) collective-permute-start(bf16[192,1024]{1,0:T(8,128)(2,1)S(1)} %broadcast_select_fusion.2), channel_id=1, source_target_pairs={{0,8},{4,12},{8,0},{12,4},{16,24},{20,28},{24,16},{28,20},{1,9},{5... | collective-permute-start | bytes 1179656 | tf_op jit(solution)/shard_map/ppermute | solution.py:515
  234.2 68.4 %collective-permute-start.17 = (bf16[512,1024]{1,0:T(8,128)(2,1)S(1)}, bf16[512,1024]{1,0:T(8,128)(2,1)}, u32[]{:S(2)}, u32[]{:S(2)}) collective-permute-start(bf16[512,1024]{1,0:T(8,128)(2,1)S(1)} %add_convert_fusion), channel_id=1, source_target_pairs={{0,2},{1,3},{2,0},{3,1},{4,6},{5,7},{6,4},{7,5},{8,10},{9,11},{10,... | collective-permute-start | bytes 3145736 | tf_op jit(solution)/shard_map/ppermute | solution.py:515
  237.3 13.0 %collective-permute-start.60 = (bf16[96,1024]{1,0:T(8,128)(2,1)S(1)}, bf16[96,1024]{1,0:T(8,128)(2,1)S(1)}, u32[]{:S(2)}, u32[]{:S(2)}) collective-permute-start(bf16[96,1024]{1,0:T(8,128)(2,1)S(1)} %broadcast_select_fusion.4), channel_id=1, source_target_pairs={{0,16},{4,20},{8,24},{12,28},{16,0},{20,4},{24,8},{28,12},{1,17},{... | collective-permute-start | bytes 589832 | tf_op jit(solution)/shard_map/ppermute | solution.py:515
  248.4 15.9 %collective-permute-start.54 = (bf16[96,1024]{1,0:T(8,128)(2,1)S(1)}, bf16[96,1024]{1,0:T(8,128)(2,1)S(1)}, u32[]{:S(2)}, u32[]{:S(2)}) collective-permute-start(bf16[96,1024]{1,0:T(8,128)(2,1)S(1)} %broadcast_select_fusion.5), channel_id=1, source_target_pairs={{0,16},{4,20},{8,24},{12,28},{16,0},{20,4},{24,8},{28,12},{1,17},{... | collective-permute-start | bytes 589832 | tf_op jit(solution)/shard_map/ppermute | solution.py:515
  250.3 22.4 %collective-permute-start.48 = (bf16[96,1024]{1,0:T(8,128)(2,1)S(1)}, bf16[96,1024]{1,0:T(8,128)(2,1)S(1)}, u32[]{:S(2)}, u32[]{:S(2)}) collective-permute-start(bf16[96,1024]{1,0:T(8,128)(2,1)S(1)} %broadcast_select_fusion.6), channel_id=1, source_target_pairs={{0,16},{4,20},{8,24},{12,28},{16,0},{20,4},{24,8},{28,12},{1,17},{... | collective-permute-start | bytes 589832 | tf_op jit(solution)/shard_map/ppermute | solution.py:515
  264.2 12.6 %collective-permute-start.61 = (bf16[96,1024]{1,0:T(8,128)(2,1)S(1)}, bf16[96,1024]{1,0:T(8,128)(2,1)S(1)}, u32[]{:S(2)}, u32[]{:S(2)}) collective-permute-start(bf16[96,1024]{1,0:T(8,128)(2,1)S(1)} %add_convert_fusion.10), channel_id=1, source_target_pairs={{0,16},{4,20},{8,24},{12,28},{16,0},{20,4},{24,8},{28,12},{1,17},{... | collective-permute-start | bytes 589832 | tf_op jit(solution)/shard_map/ppermute | solution.py:515
  272.7 12.9 %collective-permute-start.55 = (bf16[96,1024]{1,0:T(8,128)(2,1)S(1)}, bf16[96,1024]{1,0:T(8,128)(2,1)S(1)}, u32[]{:S(2)}, u32[]{:S(2)}) collective-permute-start(bf16[96,1024]{1,0:T(8,128)(2,1)S(1)} %add_convert_fusion.11), channel_id=1, source_target_pairs={{0,16},{4,20},{8,24},{12,28},{16,0},{20,4},{24,8},{28,12},{1,17},{... | collective-permute-start | bytes 589832 | tf_op jit(solution)/shard_map/ppermute | solution.py:515
  276.9 15.8 %collective-permute-start.49 = (bf16[96,1024]{1,0:T(8,128)(2,1)S(1)}, bf16[96,1024]{1,0:T(8,128)(2,1)S(1)}, u32[]{:S(2)}, u32[]{:S(2)}) collective-permute-start(bf16[96,1024]{1,0:T(8,128)(2,1)S(1)} %add_convert_fusion.12), channel_id=1, source_target_pairs={{0,16},{4,20},{8,24},{12,28},{16,0},{20,4},{24,8},{28,12},{1,17},{... | collective-permute-start | bytes 589832 | tf_op jit(solution)/shard_map/ppermute | solution.py:515
  285.6 8.3 %collective-permute-start.62 = (bf16[192,1024]{1,0:T(8,128)(2,1)S(1)}, bf16[192,1024]{1,0:T(8,128)(2,1)S(1)}, u32[]{:S(2)}, u32[]{:S(2)}) collective-permute-start(bf16[192,1024]{1,0:T(8,128)(2,1)S(1)} %maximum_select_fusion.15), channel_id=1, source_target_pairs={{0,4},{4,0},{8,12},{12,8},{16,20},{20,16},{24,28},{28,24},{1,5},{5... | collective-permute-start | bytes 1179656 | tf_op jit(solution)/shard_map/ppermute | solution.py:515
  286.2 12.3 %collective-permute-start.56 = (bf16[192,1024]{1,0:T(8,128)(2,1)S(1)}, bf16[192,1024]{1,0:T(8,128)(2,1)S(1)}, u32[]{:S(2)}, u32[]{:S(2)}) collective-permute-start(bf16[192,1024]{1,0:T(8,128)(2,1)S(1)} %maximum_select_fusion.14), channel_id=1, source_target_pairs={{0,8},{4,12},{8,0},{12,4},{16,24},{20,28},{24,16},{28,20},{1,9},{5... | collective-permute-start | bytes 1179656 | tf_op jit(solution)/shard_map/ppermute | solution.py:515
  292.7 21.8 %collective-permute-start.8 = (bf16[512,1024]{1,0:T(8,128)(2,1)}, bf16[512,1024]{1,0:T(8,128)(2,1)}, u32[]{:S(2)}, u32[]{:S(2)}) collective-permute-start(bf16[512,1024]{1,0:T(8,128)(2,1)} %get-tuple-element.57), channel_id=1, source_target_pairs={{0,1},{1,0},{2,3},{3,2},{4,5},{5,4},{6,7},{7,6},{8,9},{9,8},{10,11... | collective-permute-start | bytes 3145736 | tf_op jit(solution)/shard_map/ppermute | solution.py:515
  293.9 24.7 %collective-permute-start.14 = (bf16[512,1024]{1,0:T(8,128)(2,1)}, bf16[512,1024]{1,0:T(8,128)(2,1)}, u32[]{:S(2)}, u32[]{:S(2)}) collective-permute-start(bf16[512,1024]{1,0:T(8,128)(2,1)} %add_convert_fusion.1), channel_id=1, source_target_pairs={{0,2},{1,3},{2,0},{3,1},{4,6},{5,7},{6,4},{7,5},{8,10},{9,11},{10,... | collective-permute-start | bytes 3145736 | tf_op jit(solution)/shard_map/ppermute | solution.py:515
  298.5 12.6 %collective-permute-start.50 = (bf16[192,1024]{1,0:T(8,128)(2,1)S(1)}, bf16[192,1024]{1,0:T(8,128)(2,1)S(1)}, u32[]{:S(2)}, u32[]{:S(2)}) collective-permute-start(bf16[192,1024]{1,0:T(8,128)(2,1)S(1)} %maximum_select_fusion.13), channel_id=1, source_target_pairs={{0,8},{4,12},{8,0},{12,4},{16,24},{20,28},{24,16},{28,20},{1,9},{5... | collective-permute-start | bytes 1179656 | tf_op jit(solution)/shard_map/ppermute | solution.py:515
  302.6 23.5 %collective-permute-start.63 = (bf16[384,1024]{1,0:T(8,128)(2,1)}, bf16[384,1024]{1,0:T(8,128)(2,1)}, u32[]{:S(2)}, u32[]{:S(2)}) collective-permute-start(bf16[384,1024]{1,0:T(8,128)(2,1)} %maximum_select_fusion.7), channel_id=1, source_target_pairs={{0,8},{4,12},{8,0},{12,4},{16,24},{20,28},{24,16},{28,20},{1,9},{5... | collective-permute-start | bytes 2359304 | tf_op jit(solution)/shard_map/ppermute | solution.py:515
  307.4 20.8 %collective-permute-start.18 = (bf16[512,1024]{1,0:T(8,128)(2,1)}, bf16[512,1024]{1,0:T(8,128)(2,1)S(1)}, u32[]{:S(2)}, u32[]{:S(2)}) collective-permute-start(bf16[512,1024]{1,0:T(8,128)(2,1)} %get-tuple-element.65), channel_id=1, source_target_pairs={{0,1},{1,0},{2,3},{3,2},{4,5},{5,4},{6,7},{7,6},{8,9},{9,8},{10,11... | collective-permute-start | bytes 3145736 | tf_op jit(solution)/shard_map/ppermute | solution.py:515
  311.1 63.3 %collective-permute-start.57 = (bf16[384,1024]{1,0:T(8,128)(2,1)}, bf16[384,1024]{1,0:T(8,128)(2,1)}, u32[]{:S(2)}, u32[]{:S(2)}) collective-permute-start(bf16[384,1024]{1,0:T(8,128)(2,1)} %maximum_select_fusion.5), channel_id=1, source_target_pairs={{0,4},{4,0},{8,12},{12,8},{16,20},{20,16},{24,28},{28,24},{1,5},{5... | collective-permute-start | bytes 2359304 | tf_op jit(solution)/shard_map/ppermute | solution.py:515
  314.5 62.0 %collective-permute-start.51 = (bf16[384,1024]{1,0:T(8,128)(2,1)}, bf16[384,1024]{1,0:T(8,128)(2,1)}, u32[]{:S(2)}, u32[]{:S(2)}) collective-permute-start(bf16[384,1024]{1,0:T(8,128)(2,1)} %maximum_select_fusion.3), channel_id=1, source_target_pairs={{0,4},{4,0},{8,12},{12,8},{16,20},{20,16},{24,28},{28,24},{1,5},{5... | collective-permute-start | bytes 2359304 | tf_op jit(solution)/shard_map/ppermute | solution.py:515
  349.6 21.9 %collective-permute-start.39 = (bf16[256,1024]{1,0:T(8,128)(2,1)}, bf16[256,1024]{1,0:T(8,128)(2,1)S(1)}, u32[]{:S(2)}, u32[]{:S(2)}) collective-permute-start(bf16[256,1024]{1,0:T(8,128)(2,1)} %get-tuple-element.88), channel_id=1, source_target_pairs={{0,2},{1,3},{2,0},{3,1},{4,6},{5,7},{6,4},{7,5},{8,10},{9,11},{10,... | collective-permute-start | bytes 1572872 | tf_op jit(solution)/shard_map/ppermute | solution.py:515
  372.9 6.4 %collective-permute-start.40 = (bf16[128,1024]{1,0:T(8,128)(2,1)S(1)}, bf16[128,1024]{1,0:T(8,128)(2,1)S(1)}, u32[]{:S(2)}, u32[]{:S(2)}) collective-permute-start(bf16[128,1024]{1,0:T(8,128)(2,1)S(1)} %broadcast_select_fusion.3), channel_id=1, source_target_pairs={{0,8},{4,12},{8,0},{12,4},{16,24},{20,28},{24,16},{28,20},{1,9},{5... | collective-permute-start | bytes 786440 | tf_op jit(solution)/shard_map/ppermute | solution.py:515
  378.7 27.5 %collective-permute-start.19 = (bf16[512,1024]{1,0:T(8,128)(2,1)}, bf16[512,1024]{1,0:T(8,128)(2,1)}, u32[]{:S(2)}, u32[]{:S(2)}) collective-permute-start(bf16[512,1024]{1,0:T(8,128)(2,1)} %get-tuple-element.80), channel_id=1, source_target_pairs={{0,1},{1,0},{2,3},{3,2},{4,5},{5,4},{6,7},{7,6},{8,9},{9,8},{10,11... | collective-permute-start | bytes 3145736 | tf_op jit(solution)/shard_map/ppermute | solution.py:515
  379.5 5.4 %collective-permute-start.41 = (bf16[64,1024]{1,0:T(8,128)(2,1)S(1)}, bf16[64,1024]{1,0:T(8,128)(2,1)S(1)}, u32[]{:S(2)}, u32[]{:S(2)}) collective-permute-start(bf16[64,1024]{1,0:T(8,128)(2,1)S(1)} %broadcast_select_fusion.7), channel_id=1, source_target_pairs={{0,4},{4,0},{8,12},{12,8},{16,20},{20,16},{24,28},{28,24},{1,5},{5... | collective-permute-start | bytes 393224 | tf_op jit(solution)/shard_map/ppermute | solution.py:515
  381.8 24.2 %collective-permute-start.64 = (f32[1,256]{1,0:T(1,128)S(1)}, f32[1,256]{1,0:T(1,128)S(1)}, u32[]{:S(2)}, u32[]{:S(2)}) collective-permute-start(f32[1,256]{1,0:T(1,128)S(1)} %copy-done.29), channel_id=1, source_target_pairs={{0,2},{1,3},{2,0},{3,1},{4,6},{5,7},{6,4},{7,5},{8,10},{9,11},{10,... | collective-permute-start | bytes 3080 | tf_op jit(solution)/shard_map/ppermute | solution.py:515
  384.9 21.1 %collective-permute-start.42 = (bf16[32,1024]{1,0:T(8,128)(2,1)S(1)}, bf16[32,1024]{1,0:T(8,128)(2,1)S(1)}, u32[]{:S(2)}, u32[]{:S(2)}) collective-permute-start(bf16[32,1024]{1,0:T(8,128)(2,1)S(1)} %broadcast_select_fusion.11), channel_id=1, source_target_pairs={{0,16},{4,20},{8,24},{12,28},{16,0},{20,4},{24,8},{28,12},{1,17},{... | collective-permute-start | bytes 196616 | tf_op jit(solution)/shard_map/ppermute | solution.py:515
  405.7 37.2 %collective-permute-start.20 = (bf16[3,1024,256]{2,1,0:T(8,128)(2,1)}, bf16[3,1024,256]{2,1,0:T(8,128)(2,1)}, u32[]{:S(2)}, u32[]{:S(2)}) collective-permute-start(bf16[3,1024,256]{2,1,0:T(8,128)(2,1)} %get-tuple-element.86), channel_id=1, source_target_pairs={{0,2},{1,3},{2,0},{3,1},{4,6},{5,7},{6,4},{7,5},{8,10},{9,11},{10,... | collective-permute-start | bytes 4718600 | tf_op jit(solution)/shard_map/ppermute | solution.py:515
  406.1 10.7 %collective-permute-start.43 = (bf16[32,1024]{1,0:T(8,128)(2,1)S(1)}, bf16[32,1024]{1,0:T(8,128)(2,1)S(1)}, u32[]{:S(2)}, u32[]{:S(2)}) collective-permute-start(bf16[32,1024]{1,0:T(8,128)(2,1)S(1)} %add_convert_fusion.17), channel_id=1, source_target_pairs={{0,16},{4,20},{8,24},{12,28},{16,0},{20,4},{24,8},{28,12},{1,17},{... | collective-permute-start | bytes 196616 | tf_op jit(solution)/shard_map/ppermute | solution.py:515
  416.8 7.7 %collective-permute-start.44 = (bf16[64,1024]{1,0:T(8,128)(2,1)S(1)}, bf16[64,1024]{1,0:T(8,128)(2,1)S(1)}, u32[]{:S(2)}, u32[]{:S(2)}) collective-permute-start(bf16[64,1024]{1,0:T(8,128)(2,1)S(1)} %maximum_select_fusion.23), channel_id=1, source_target_pairs={{0,4},{4,0},{8,12},{12,8},{16,20},{20,16},{24,28},{28,24},{1,5},{5... | collective-permute-start | bytes 393224 | tf_op jit(solution)/shard_map/ppermute | solution.py:515
  420.0 7.8 %collective-permute-start.67 = (f32[4,8,1024]{2,0,1:T(4,128)S(1)}, f32[4,8,1024]{2,0,1:T(4,128)S(1)}, u32[]{:S(2)}, u32[]{:S(2)}) collective-permute-start(f32[4,8,1024]{2,0,1:T(4,128)S(1)} %pad_maximum_fusion.2), channel_id=1, source_target_pairs={{0,16},{4,20},{8,24},{12,28},{16,0},{20,4},{24,8},{28,12},{1,17},{... | collective-permute-start | bytes 393224 | tf_op jit(solution)/shard_map/ppermute | solution.py:515
  424.6 7.9 %collective-permute-start.45 = (bf16[128,1024]{1,0:T(8,128)(2,1)S(1)}, bf16[128,1024]{1,0:T(8,128)(2,1)S(1)}, u32[]{:S(2)}, u32[]{:S(2)}) collective-permute-start(bf16[128,1024]{1,0:T(8,128)(2,1)S(1)} %maximum_select_fusion.19), channel_id=1, source_target_pairs={{0,8},{4,12},{8,0},{12,4},{16,24},{20,28},{24,16},{28,20},{1,9},{5... | collective-permute-start | bytes 786440 | tf_op jit(solution)/shard_map/ppermute | solution.py:515
  430.9 18.7 %collective-permute-start.69 = (bf16[16,8,1024]{2,0,1:T(8,128)(2,1)}, bf16[16,8,1024]{2,0,1:T(8,128)(2,1)}, u32[]{:S(2)}, u32[]{:S(2)}) collective-permute-start(bf16[16,8,1024]{2,0,1:T(8,128)(2,1)} %concatenate.438), channel_id=1, source_target_pairs={{0,2},{1,3},{2,0},{3,1},{4,6},{5,7},{6,4},{7,5},{8,10},{9,11},{10,... | collective-permute-start | bytes 786440 | tf_op jit(solution)/shard_map/ppermute | solution.py:515
  445.8 10.4 %collective-permute-start.33 = (bf16[512,256]{1,0:T(8,128)(2,1)}, bf16[512,256]{1,0:T(8,128)(2,1)}, u32[]{:S(2)}, u32[]{:S(2)}) collective-permute-start(bf16[512,256]{1,0:T(8,128)(2,1)} %select_bitcast_fusion.3), channel_id=1, source_target_pairs={{0,4},{4,0},{8,12},{12,8},{16,20},{20,16},{24,28},{28,24},{1,5},{5... | collective-permute-start | bytes 786440 | tf_op jit(solution)/shard_map/ppermute | solution.py:515
  446.8 10.8 %collective-permute-start.27 = (bf16[512,256]{1,0:T(8,128)(2,1)}, bf16[512,256]{1,0:T(8,128)(2,1)}, u32[]{:S(2)}, u32[]{:S(2)}) collective-permute-start(bf16[512,256]{1,0:T(8,128)(2,1)} %select_bitcast_fusion.4), channel_id=1, source_target_pairs={{0,4},{4,0},{8,12},{12,8},{16,20},{20,16},{24,28},{28,24},{1,5},{5... | collective-permute-start | bytes 786440 | tf_op jit(solution)/shard_map/ppermute | solution.py:515
  449.3 11.2 %collective-permute-start.21 = (bf16[512,256]{1,0:T(8,128)(2,1)}, bf16[512,256]{1,0:T(8,128)(2,1)}, u32[]{:S(2)}, u32[]{:S(2)}) collective-permute-start(bf16[512,256]{1,0:T(8,128)(2,1)} %select_bitcast_fusion.5), channel_id=1, source_target_pairs={{0,4},{4,0},{8,12},{12,8},{16,20},{20,16},{24,28},{28,24},{1,5},{5... | collective-permute-start | bytes 786440 | tf_op jit(solution)/shard_map/ppermute | solution.py:515
  458.8 6.4 %collective-permute-start.28 = (bf16[256,256]{1,0:T(8,128)(2,1)S(1)}, bf16[256,256]{1,0:T(8,128)(2,1)S(1)}, u32[]{:S(2)}, u32[]{:S(2)}) collective-permute-start(bf16[256,256]{1,0:T(8,128)(2,1)S(1)} %broadcast_select_fusion.9), channel_id=1, source_target_pairs={{0,8},{4,12},{8,0},{12,4},{16,24},{20,28},{24,16},{28,20},{1,9},{5... | collective-permute-start | bytes 393224 | tf_op jit(solution)/shard_map/ppermute | solution.py:515
  461.6 6.1 %collective-permute-start.22 = (bf16[256,256]{1,0:T(8,128)(2,1)S(1)}, bf16[256,256]{1,0:T(8,128)(2,1)S(1)}, u32[]{:S(2)}, u32[]{:S(2)}) collective-permute-start(bf16[256,256]{1,0:T(8,128)(2,1)S(1)} %broadcast_select_fusion.10), channel_id=1, source_target_pairs={{0,8},{4,12},{8,0},{12,4},{16,24},{20,28},{24,16},{28,20},{1,9},{5... | collective-permute-start | bytes 393224 | tf_op jit(solution)/shard_map/ppermute | solution.py:515
  462.4 7.4 %collective-permute-start.35 = (bf16[128,256]{1,0:T(8,128)(2,1)S(1)}, bf16[128,256]{1,0:T(8,128)(2,1)S(1)}, u32[]{:S(2)}, u32[]{:S(2)}) collective-permute-start(bf16[128,256]{1,0:T(8,128)(2,1)S(1)} %broadcast_select_fusion.12), channel_id=1, source_target_pairs={{0,16},{4,20},{8,24},{12,28},{16,0},{20,4},{24,8},{28,12},{1,17},{... | collective-permute-start | bytes 196616 | tf_op jit(solution)/shard_map/ppermute | solution.py:515
  465.2 6.8 %collective-permute-start.29 = (bf16[128,256]{1,0:T(8,128)(2,1)S(1)}, bf16[128,256]{1,0:T(8,128)(2,1)S(1)}, u32[]{:S(2)}, u32[]{:S(2)}) collective-permute-start(bf16[128,256]{1,0:T(8,128)(2,1)S(1)} %broadcast_select_fusion.13), channel_id=1, source_target_pairs={{0,16},{4,20},{8,24},{12,28},{16,0},{20,4},{24,8},{28,12},{1,17},{... | collective-permute-start | bytes 196616 | tf_op jit(solution)/shard_map/ppermute | solution.py:515
  467.8 5.6 %collective-permute-start.23 = (bf16[128,256]{1,0:T(8,128)(2,1)S(1)}, bf16[128,256]{1,0:T(8,128)(2,1)S(1)}, u32[]{:S(2)}, u32[]{:S(2)}) collective-permute-start(bf16[128,256]{1,0:T(8,128)(2,1)S(1)} %broadcast_select_fusion.14), channel_id=1, source_target_pairs={{0,16},{4,20},{8,24},{12,28},{16,0},{20,4},{24,8},{28,12},{1,17},{... | collective-permute-start | bytes 196616 | tf_op jit(solution)/shard_map/ppermute | solution.py:515
  469.9 6.2 %collective-permute-start.36 = (bf16[128,256]{1,0:T(8,128)(2,1)S(1)}, bf16[128,256]{1,0:T(8,128)(2,1)S(1)}, u32[]{:S(2)}, u32[]{:S(2)}) collective-permute-start(bf16[128,256]{1,0:T(8,128)(2,1)S(1)} %add_convert_fusion.18), channel_id=1, source_target_pairs={{0,16},{4,20},{8,24},{12,28},{16,0},{20,4},{24,8},{28,12},{1,17},{... | collective-permute-start | bytes 196616 | tf_op jit(solution)/shard_map/ppermute | solution.py:515
  472.0 5.9 %collective-permute-start.30 = (bf16[128,256]{1,0:T(8,128)(2,1)S(1)}, bf16[128,256]{1,0:T(8,128)(2,1)S(1)}, u32[]{:S(2)}, u32[]{:S(2)}) collective-permute-start(bf16[128,256]{1,0:T(8,128)(2,1)S(1)} %add_convert_fusion.19), channel_id=1, source_target_pairs={{0,16},{4,20},{8,24},{12,28},{16,0},{20,4},{24,8},{28,12},{1,17},{... | collective-permute-start | bytes 196616 | tf_op jit(solution)/shard_map/ppermute | solution.py:515
  473.4 5.2 %collective-permute-start.24 = (bf16[128,256]{1,0:T(8,128)(2,1)S(1)}, bf16[128,256]{1,0:T(8,128)(2,1)S(1)}, u32[]{:S(2)}, u32[]{:S(2)}) collective-permute-start(bf16[128,256]{1,0:T(8,128)(2,1)S(1)} %add_convert_fusion.20), channel_id=1, source_target_pairs={{0,16},{4,20},{8,24},{12,28},{16,0},{20,4},{24,8},{28,12},{1,17},{... | collective-permute-start | bytes 196616 | tf_op jit(solution)/shard_map/ppermute | solution.py:515
  477.9 5.2 %collective-permute-start.31 = (bf16[256,256]{1,0:T(8,128)(2,1)S(1)}, bf16[256,256]{1,0:T(8,128)(2,1)S(1)}, u32[]{:S(2)}, u32[]{:S(2)}) collective-permute-start(bf16[256,256]{1,0:T(8,128)(2,1)S(1)} %maximum_select_fusion.21), channel_id=1, source_target_pairs={{0,8},{4,12},{8,0},{12,4},{16,24},{20,28},{24,16},{28,20},{1,9},{5... | collective-permute-start | bytes 393224 | tf_op jit(solution)/shard_map/ppermute | solution.py:515
  478.7 6.4 %collective-permute-start.25 = (bf16[256,256]{1,0:T(8,128)(2,1)S(1)}, bf16[256,256]{1,0:T(8,128)(2,1)S(1)}, u32[]{:S(2)}, u32[]{:S(2)}) collective-permute-start(bf16[256,256]{1,0:T(8,128)(2,1)S(1)} %maximum_select_fusion.20), channel_id=1, source_target_pairs={{0,8},{4,12},{8,0},{12,4},{16,24},{20,28},{24,16},{28,20},{1,9},{5... | collective-permute-start | bytes 393224 | tf_op jit(solution)/shard_map/ppermute | solution.py:515
  481.2 8.5 %collective-permute-start.38 = (bf16[512,256]{1,0:T(8,128)(2,1)S(1)}, bf16[512,256]{1,0:T(8,128)(2,1)S(1)}, u32[]{:S(2)}, u32[]{:S(2)}) collective-permute-start(bf16[512,256]{1,0:T(8,128)(2,1)S(1)} %maximum_select_fusion.18), channel_id=1, source_target_pairs={{0,4},{4,0},{8,12},{12,8},{16,20},{20,16},{24,28},{28,24},{1,5},{5... | collective-permute-start | bytes 786440 | tf_op jit(solution)/shard_map/ppermute | solution.py:515
  483.2 7.2 %collective-permute-start.32 = (bf16[512,256]{1,0:T(8,128)(2,1)S(1)}, bf16[512,256]{1,0:T(8,128)(2,1)S(1)}, u32[]{:S(2)}, u32[]{:S(2)}) collective-permute-start(bf16[512,256]{1,0:T(8,128)(2,1)S(1)} %maximum_select_fusion.17), channel_id=1, source_target_pairs={{0,4},{4,0},{8,12},{12,8},{16,20},{20,16},{24,28},{28,24},{1,5},{5... | collective-permute-start | bytes 786440 | tf_op jit(solution)/shard_map/ppermute | solution.py:515
  485.2 8.1 %collective-permute-start.26 = (bf16[512,256]{1,0:T(8,128)(2,1)S(1)}, bf16[512,256]{1,0:T(8,128)(2,1)S(1)}, u32[]{:S(2)}, u32[]{:S(2)}) collective-permute-start(bf16[512,256]{1,0:T(8,128)(2,1)S(1)} %maximum_select_fusion.16), channel_id=1, source_target_pairs={{0,4},{4,0},{8,12},{12,8},{16,20},{20,16},{24,28},{28,24},{1,5},{5... | collective-permute-start | bytes 786440 | tf_op jit(solution)/shard_map/ppermute | solution.py:515
  (38 other events, 363.6 us)
